TPU v7x, 256 devices: a whole 4x4x8 slice. The times are simulated.
256 devices in a mesh: flow: 16 (over y_lo, x, core), span: 16 (over y_hi, z).
Axes of the slice: x: 4, y: 4 (y_hi: 2, y_lo: 2; y = y_hi * 2 + y_lo), z: 8, core: 2. Of those that a mesh axis runs over, the one named last changes fastest.
Arguments:
- populations: float32 [19, 256, 256, 128], P(None, 'flow', 'span'), as said below
- gray: float32 [256, 256, 128], P('flow', 'span'), may hold values from 0 to 0.6
- fluid_mask: int32 [256, 256, 128], P('flow', 'span'), may hold values from 0 to 1, as said below
- cotangent: float32 [19, 256, 256, 128], P(None, 'flow', 'span'), may hold values from -6 to 6
Outputs:
- initial_adjoint: float32 [19, 256, 256, 128], P(None, 'flow', 'span')
- profile: float32 [256], P('flow')
Inputs may be any that keep to these rules, and one draw needn't show every extreme that they name: populations are positive, each within 40 percent of an equilibrium at a density of 0.7 to 1.3 with velocity components under 0.1. fluid_mask is 0 throughout rock tiles, the aligned cubes of 16 x 16 x 16 voxels that hold no pore; how many tiles of one device's block hold pore differs from block to block.
All inputs are finite; a program needn't handle non-finite values.
Results may differ from a plain program's by a relative error of at most 0.0003.
Values sent between devices are 32-bit elements; how exact they have to be, the bound alone decides.
A program may use at most 128 MiB of HBM per device.

v0:
```python
import functools
import math

import jax
import jax.numpy as jnp
from jax import lax
from jax.experimental import pallas as pl
from jax.experimental.pallas import tpu as pltpu
from jax.sharding import PartitionSpec as P

VELOCITY = (
    (0, 0, 0),
    (1, 0, 0), (-1, 0, 0), (0, 1, 0), (0, -1, 0), (0, 0, 1), (0, 0, -1),
    (1, 1, 0), (-1, -1, 0), (1, -1, 0), (-1, 1, 0),
    (1, 0, 1), (-1, 0, -1), (1, 0, -1), (-1, 0, 1),
    (0, 1, 1), (0, -1, -1), (0, 1, -1), (0, -1, 1),
)
ORDER = (1, 7, 9, 11, 13, 2, 8, 10, 12, 14, 0, 3, 4, 5, 6, 15, 16, 17, 18)
SLOT = tuple(ORDER.index(i) for i in range(19))
X_GROUP = {1: 0, -1: 5}
Y_GROUP = {s: tuple(i for i in range(19) if VELOCITY[i][1] == s) for s in (1, -1)}
CORNER = {(1, 1): 7, (-1, -1): 8, (1, -1): 9, (-1, 1): 10}
CORNERS = ((1, 1), (-1, -1), (1, -1), (-1, 1))
PAIRS = ((1, 2), (3, 4), (5, 6), (7, 8), (9, 10), (11, 12), (13, 14), (15, 16), (17, 18))
RATE = 1.0 / 0.6 - 1.2
PITCH = 32
BASE = 8
NX = 16
NY = 16
NZ = 128


def split(f):
    even = [f[p] + f[m] for p, m in PAIRS]
    odd = [f[p] - f[m] for p, m in PAIRS]
    return even, odd


def sums(even, odd):
    plane = [even[3 + 2 * k] + even[4 + 2 * k] for k in range(3)]
    cross = [even[3 + 2 * k] - even[4 + 2 * k] for k in range(3)]
    plus = [odd[3 + 2 * k] + odd[4 + 2 * k] for k in range(3)]
    minus = [odd[3 + 2 * k] - odd[4 + 2 * k] for k in range(3)]
    first = [plus[0] + plus[1], minus[0] + plus[2], minus[1] + minus[2]]
    return plane, cross, first


def state_of(f):
    even, odd = split(f)
    plane, cross, first = sums(even, odd)
    j = [odd[a] + first[a] for a in range(3)]
    second = [even[0] + (plane[0] + plane[1]), even[1] + (plane[0] + plane[2]), even[2] + (plane[1] + plane[2])]
    rho = (f[0] + second[0]) + (even[1] + even[2]) + plane[2]
    inv = 1.0 / rho
    u = [entry * inv for entry in j]
    return even, odd, cross, j, second, rho, u


def join(even, odd):
    out = [None] * 19
    for k, (p, m) in enumerate(PAIRS):
        out[p] = even[k] + odd[k]
        out[m] = even[k] - odd[k]
    return out


def collide(f, share):
    even, odd, cross, j, second, rho, u = state_of(f)
    keep = 1.0 - share
    k_even = 0.6 * share - 0.1
    k_odd = -0.4 * share - 0.1
    square = [j[a] * u[a] for a in range(3)]
    mixed = [j[0] * u[1], j[0] * u[2], j[1] * u[2]]
    base = rho - 1.5 * (square[0] + square[1] + square[2])
    third = rho * (1.0 / 3.0)
    lack = [second[a] - third - square[a] for a in range(3)]
    rest = 0.4 * base + RATE * (lack[0] + lack[1] + lack[2])
    base_axis = base * (1.0 / 15.0)
    base_edge = base * (1.0 / 30.0)
    grown = [0.15 * square[a] for a in range(3)]
    e_parts = [base_axis + 2.0 * grown[a] - (0.5 * RATE) * lack[a] for a in range(3)]
    ends = ((0, 1), (0, 2), (1, 2))
    o_parts = [0.2 * j[a] for a in range(3)]
    half = [0.1 * j[a] for a in range(3)]
    for k, (a, b) in enumerate(ends):
        common = base_edge + (grown[a] + grown[b])
        twist = (5.0 / 12.0) * mixed[k] - (0.25 * RATE) * cross[k]
        e_parts += [common + twist, common - twist]
        o_parts += [half[a] + half[b], half[a] - half[b]]
    out_even = [k_even * even[k] + keep * e_parts[k] for k in range(9)]
    out_odd = [k_odd * odd[k] + keep * o_parts[k] for k in range(9)]
    out = join(out_even, out_odd)
    out[0] = 2.0 * (k_even * f[0]) + keep * rest
    return out


def pull_back(f, g, share):
    even, odd, cross, j, second, rho, u = state_of(f)
    g_even, g_odd = split(g)
    g_plane, g_cross, g_first = sums(g_even, g_odd)
    keep = 1.0 - share
    k_even = 0.6 * share - 0.1
    k_odd = -0.4 * share - 0.1
    ends = ((0, 1), (0, 2), (1, 2))
    g_axes = g_even[0] + g_even[1] + g_even[2]
    g_edges = g_plane[0] + g_plane[1] + g_plane[2]
    weighted = g[0] * (1.0 / 3.0) + g_axes * (1.0 / 18.0) + g_edges * (1.0 / 36.0)
    both = [g_plane[0] + g_plane[1], g_plane[0] + g_plane[2], g_plane[1] + g_plane[2]]
    diag = [0.5 * g_even[a] - g[0] for a in range(3)]
    side = [0.25 * g_cross[k] for k in range(3)]
    flow = [0.2 * g_odd[a] + 0.1 * g_first[a] for a in range(3)]
    shared = 3.6 * weighted
    entry = [0.6 * g_even[a] + 0.3 * both[a] + (2.0 * RATE) * diag[a] - shared for a in range(3)]
    tilt = [(5.0 / 3.0) * side[k] for k in range(3)]
    turn = [
        u[0] * entry[0] + (tilt[0] * u[1] + tilt[1] * u[2]),
        u[1] * entry[1] + (tilt[0] * u[0] + tilt[2] * u[2]),
        u[2] * entry[2] + (tilt[1] * u[0] + tilt[2] * u[1]),
    ]
    scalar = 1.2 * weighted + (RATE / 3.0) * (diag[0] + diag[1] + diag[2])
    half_turn = [0.5 * turn[a] for a in range(3)]
    bar_rho = scalar - (u[0] * half_turn[0] + u[1] * half_turn[1] + u[2] * half_turn[2])
    grade = 1.2 * (g[0] * f[0]) - rho * scalar
    for a in range(3):
        grade = grade - j[a] * (flow[a] + half_turn[a])
    bend = diag[0] * second[0] + diag[1] * second[1] + diag[2] * second[2]
    bend = bend + side[0] * cross[0] + side[1] * cross[1] + side[2] * cross[2]
    dot_even = g_even[0] * even[0]
    dot_odd = g_odd[0] * odd[0]
    for k in range(1, 9):
        dot_even = dot_even + g_even[k] * even[k]
        dot_odd = dot_odd + g_odd[k] * odd[k]
    grade = grade + RATE * bend + (0.6 * dot_even - 0.4 * dot_odd)
    bar_rho = keep * bar_rho
    bar_j = [keep * (flow[a] + turn[a]) for a in range(3)]
    scale = keep * RATE
    diag = [scale * entry_a for entry_a in diag]
    side = [scale * entry_k for entry_k in side]
    e_parts = [bar_rho - diag[a] for a in range(3)]
    o_parts = list(bar_j)
    for k, (a, b) in enumerate(ends):
        common = e_parts[a] - diag[b]
        e_parts += [common - side[k], common + side[k]]
        o_parts += [bar_j[a] + bar_j[b], bar_j[a] - bar_j[b]]
    out = join(
        [k_even * g_even[k] + e_parts[k] for k in range(9)],
        [k_odd * g_odd[k] + o_parts[k] for k in range(9)],
    )
    out[0] = 2.0 * (k_even * g[0]) + bar_rho
    return out, grade


def lane_shift(value, step, lane):
    if step == 0:
        return value
    if step > 0:
        return jnp.where(lane == 0, 0.0, pltpu.roll(value, 1, 1))
    return jnp.where(lane == NZ - 1, 0.0, pltpu.roll(value, NZ - 1, 1))


def kernel(
    flows, spans,
    pop_hbm, gray_hbm, mask_hbm, cot_hbm,
    out_ref, profile_ref,
    pop, gray, mask, post, cot, pre,
    y_send, y_recv, c_recv, grade_sum, rows,
    in_sems, send_sems, recv_sems, row_send, row_recv,
):
    fl = lax.axis_index("flow")
    sp = lax.axis_index("span")
    up = lax.rem(fl + 1, flows)
    down = lax.rem(fl + flows - 1, flows)
    flow_at = {1: up, -1: down}
    span_at = {1: sp + 1, -1: sp - 1}
    inside = {1: sp < spans - 1, -1: sp > 0}

    def target(step_x, step_y):
        return {
            "flow": flow_at[step_x] if step_x else fl,
            "span": span_at[step_y] if step_y else sp,
        }

    loads = [
        pltpu.make_async_copy(pop_hbm, pop, in_sems.at[0]),
        pltpu.make_async_copy(gray_hbm, gray, in_sems.at[1]),
        pltpu.make_async_copy(mask_hbm, mask, in_sems.at[2]),
    ]
    for load in loads:
        load.start()
    cot_loads = [
        pltpu.make_async_copy(
            cot_hbm.at[ORDER[k]], cot.at[k, pl.ds(1, NX), pl.ds(BASE, NY), :], in_sems.at[3 + k]
        )
        for k in range(19)
    ]
    for load in cot_loads:
        load.start()

    barrier = pltpu.get_barrier_semaphore()
    for step in range(1, spans):
        pl.semaphore_signal(barrier, inc=1, device_id={"flow": fl, "span": lax.rem(sp + step, spans)})
    for step_x in (1, -1):
        pl.semaphore_signal(barrier, inc=1, device_id=target(step_x, 0))
        for step_y in (1, -1):

            @pl.when(inside[step_y])
            def _():
                pl.semaphore_signal(barrier, inc=1, device_id=target(step_x, step_y))

    count = spans + 1 + 2 * (sp > 0).astype(jnp.int32) + 2 * (sp < spans - 1).astype(jnp.int32)
    pl.semaphore_wait(barrier, count)

    def remote(src, dst, turn, index, where):
        return pltpu.make_async_remote_copy(
            src_ref=src,
            dst_ref=dst,
            send_sem=send_sems.at[turn, index],
            recv_sem=recv_sems.at[turn, index],
            device_id=where,
        )

    def copies(buf, sign, turn):
        made = []
        for n, step in enumerate((1, -1)):
            first = X_GROUP[sign * step]
            made.append((
                remote(
                    buf.at[pl.ds(first, 5), NX if step > 0 else 1, pl.ds(BASE, NY), :],
                    buf.at[pl.ds(first, 5), 0 if step > 0 else NX + 1, pl.ds(BASE, NY), :],
                    turn, n, target(step, 0),
                ), None, None,
            ))
        for n, step in enumerate((1, -1)):
            made.append((
                remote(y_send.at[turn, n], y_recv.at[turn, n], turn, 2 + n, target(0, step)),
                inside[step], inside[-step],
            ))
        for n, (step_x, step_y) in enumerate(CORNERS):
            slot = SLOT[CORNER[(sign * step_x, sign * step_y)]]
            made.append((
                remote(
                    buf.at[slot, NX if step_x > 0 else 1, pl.ds(BASE + (8 if step_y > 0 else 0), 8), :],
                    c_recv.at[turn, n], turn, 4 + n, target(step_x, step_y),
                ), inside[step_y], inside[-step_y],
            ))
        return made

    def send(buf, sign, turn):
        flat = buf.reshape(19, (NX + 2) * PITCH, NZ)
        for n, step in enumerate((1, -1)):
            row = PITCH + BASE + (NY - 1 if step > 0 else 0)
            for k, i in enumerate(Y_GROUP[sign * step]):
                y_send[turn, n, k] = flat[SLOT[i], pl.ds(row, NX, stride=PITCH), :]
        made = copies(buf, sign, turn)
        for copy, sent, _ in made:
            if sent is None:
                copy.start()
            else:
                pl.when(sent)(copy.start)
        return made

    def receive(made, buf, sign, turn):
        flat = buf.reshape(19, (NX + 2) * PITCH, NZ)
        for copy, _, received in made:
            if received is None:
                copy.wait_recv()
            else:
                pl.when(received)(copy.wait_recv)
        for n, step in enumerate((1, -1)):
            row = PITCH + BASE + (-1 if step > 0 else NY)

            def place(step=step, n=n, row=row, empty=False):
                for k, i in enumerate(Y_GROUP[sign * step]):
                    value = jnp.zeros((NX, NZ), jnp.float32) if empty else y_recv[turn, n, k]
                    flat[SLOT[i], pl.ds(row, NX, stride=PITCH), :] = value
                for m, (step_x, step_y) in enumerate(CORNERS):
                    if step_y != step:
                        continue
                    slot = SLOT[CORNER[(sign * step_x, sign * step_y)]]
                    at = 7 if step_y > 0 else 0
                    corner = jnp.zeros((1, NZ), jnp.float32) if empty else c_recv[turn, m, pl.ds(at, 1), :]
                    plane = 0 if step_x > 0 else NX + 1
                    flat[slot, pl.ds(plane * PITCH + BASE + (-1 if step > 0 else NY), 1), :] = corner

            pl.when(inside[-step])(place)
            pl.when(jnp.logical_not(inside[-step]))(functools.partial(place, empty=True))

    def finish(made):
        for copy, sent, _ in made:
            if sent is None:
                copy.wait_send()
            else:
                pl.when(sent)(copy.wait_send)

    lane = lax.broadcasted_iota(jnp.int32, (8, NZ), 1)

    def share_at(x, h):
        return jnp.where(mask[x, pl.ds(8 * h, 8), :] == 1, gray[x, pl.ds(8 * h, 8), :], 1.0)

    def moved(buf, x, h, sign):
        return [
            buf[
                SLOT[i],
                x + 1 - sign * VELOCITY[i][0],
                pl.ds(BASE + 8 * h - sign * VELOCITY[i][1], 8),
                :,
            ]
            for i in range(19)
        ]

    def store_moved(buf, x, h, values, sign):
        for i in range(19):
            buf[SLOT[i], x + 1, pl.ds(BASE + 8 * h, 8), :] = lane_shift(values[i], sign * VELOCITY[i][2], lane)

    for load in loads:
        load.wait()

    @pl.loop(0, NX)
    def _(x):
        for h in range(2):
            f = [pop[i, x, pl.ds(8 * h, 8), :] for i in range(19)]
            store_moved(post, x, h, collide(f, share_at(x, h)), 1)

    post_copies = send(post, 1, 0)
    for load in cot_loads:
        load.wait()
    cot_copies = send(cot, -1, 1)
    receive(cot_copies, cot, -1, 1)
    receive(post_copies, post, 1, 0)

    @pl.loop(0, NX)
    def _(x):
        total = None
        for h in range(2):
            f = moved(post, x, h, 1)
            g = [lane_shift(value, -VELOCITY[i][2], lane) for i, value in enumerate(moved(cot, x, h, -1))]
            out, grade = pull_back(f, g, share_at(x, h))
            store_moved(pre, x, h, out, -1)
            grade = jnp.where(mask[x, pl.ds(8 * h, 8), :] == 1, grade, 0.0)
            total = grade if total is None else total + grade
        grade_sum[x] = total

    pre_copies = send(pre, -1, 2)
    receive(pre_copies, pre, -1, 2)

    @pl.loop(0, NX)
    def _(x):
        total = grade_sum[x]
        for h in range(2):
            f = [pop[i, x, pl.ds(8 * h, 8), :] for i in range(19)]
            out, grade = pull_back(f, moved(pre, x, h, -1), share_at(x, h))
            for i in range(19):
                out_ref[i, x, pl.ds(8 * h, 8), :] = out[i]
            total = total + jnp.where(mask[x, pl.ds(8 * h, 8), :] == 1, grade, 0.0)
        grade_sum[x] = total

    partial = jnp.sum(grade_sum[...], axis=1)
    partial = jnp.sum(partial, axis=1, keepdims=True)
    wide = (NX, NZ)
    at_row = lax.broadcasted_iota(jnp.int32, wide, 0) == lax.broadcasted_iota(jnp.int32, wide, 1)
    rows[sp] = jnp.sum(jnp.where(at_row, partial, 0.0), axis=0, keepdims=True)
    row_copies = []
    for step in range(1, spans):
        copy = pltpu.make_async_remote_copy(
            src_ref=rows.at[sp],
            dst_ref=rows.at[sp],
            send_sem=row_send.at[step],
            recv_sem=row_recv.at[step],
            device_id={"flow": fl, "span": lax.rem(sp + step, spans)},
        )
        copy.start()
        row_copies.append(copy)
    finish(post_copies)
    finish(cot_copies)
    finish(pre_copies)
    for copy in row_copies:
        copy.wait_recv()
    total = rows[0]
    for step in range(1, spans):
        total = total + rows[step]
    total = total * (1.0 / math.sqrt(spans * NY * NZ))
    profile_ref[...] = total[:, :NX]
    for copy in row_copies:
        copy.wait_send()


def local(flows, spans, populations, gray, fluid_mask, cotangent):
    padded = pltpu.VMEM((19, NX + 2, PITCH, NZ), jnp.float32)
    block = pltpu.VMEM((19, NX, NY, NZ), jnp.float32)
    adjoint, profile = pl.pallas_call(
        functools.partial(kernel, flows, spans),
        out_shape=(
            jax.ShapeDtypeStruct((19, NX, NY, NZ), jnp.float32),
            jax.ShapeDtypeStruct((1, NX), jnp.float32),
        ),
        in_specs=[pl.BlockSpec(memory_space=pl.ANY)] * 4,
        out_specs=(pl.BlockSpec(memory_space=pltpu.VMEM), pl.BlockSpec(memory_space=pltpu.VMEM)),
        scratch_shapes=[
            block,
            pltpu.VMEM((NX, NY, NZ), jnp.float32),
            pltpu.VMEM((NX, NY, NZ), jnp.int32),
            padded,
            padded,
            padded,
            pltpu.VMEM((3, 2, 5, NX, NZ), jnp.float32),
            pltpu.VMEM((3, 2, 5, NX, NZ), jnp.float32),
            pltpu.VMEM((3, 4, 8, NZ), jnp.float32),
            pltpu.VMEM((NX, 8, NZ), jnp.float32),
            pltpu.VMEM((spans, 1, NZ), jnp.float32),
            pltpu.SemaphoreType.DMA((22,)),
            pltpu.SemaphoreType.DMA((3, 8)),
            pltpu.SemaphoreType.DMA((3, 8)),
            pltpu.SemaphoreType.DMA((spans,)),
            pltpu.SemaphoreType.DMA((spans,)),
        ],
        compiler_params=pltpu.CompilerParams(
            collective_id=0, has_side_effects=True, vmem_limit_bytes=44 * 1024 * 1024
        ),
    )(populations, gray, fluid_mask, cotangent)
    return adjoint, profile.reshape(NX)


def solution(mesh):
    placed = (
        P(None, "flow", "span", None),
        P("flow", "span", None),
        P("flow", "span", None),
        P(None, "flow", "span", None),
    )
    return jax.shard_map(
        functools.partial(local, mesh.shape["flow"], mesh.shape["span"]),
        mesh=mesh,
        in_specs=placed,
        out_specs=(P(None, "flow", "span", None), P("flow")),
        check_vma=False,
    )
```

profile of v0, /device:TPU:1, one launch (start us, length us, event | category | flops | bytes accessed | tf_op | source)
XLA Modules:
  0.0 41.9 jit_solution(3209186359008610807)
XLA Ops:
  0.6 0.0 copy-start
  0.6 1.7 %copy-done = f32[19,16,16,128]{3,2,1,0:T(8,128)S(1)} copy-done((f32[19,16,16,128]{3,2,1,0:T(8,128)S(1)}, f32[19,16,16,128]{3,2,1,0:T(8,128)}, u32[]{:S(2)}) %copy-start) | copy-done | bytes 2490392
  2.3 0.0 copy-start.1
  2.3 1.7 %copy-done.1 = f32[19,16,16,128]{3,2,1,0:T(8,128)S(1)} copy-done((f32[19,16,16,128]{3,2,1,0:T(8,128)S(1)}, f32[19,16,16,128]{3,2,1,0:T(8,128)}, u32[]{:S(2)}) %copy-start.1) | copy-done | bytes 2490392
  4.0 0.0 copy-start.2
  4.0 0.9 %copy-done.2 = f32[16,16,128]{2,1,0:T(8,128)S(1)} copy-done((f32[16,16,128]{2,1,0:T(8,128)S(1)}, f32[16,16,128]{2,1,0:T(8,128)}, u32[]{:S(2)}) %copy-start.2) | copy-done | bytes 131096
  4.9 0.0 copy-start.3
  4.9 0.9 %copy-done.3 = s32[16,16,128]{2,1,0:T(8,128)S(1)} copy-done((s32[16,16,128]{2,1,0:T(8,128)S(1)}, s32[16,16,128]{2,1,0:T(8,128)}, u32[]{:S(2)}) %copy-start.3) | copy-done | bytes 131096
  5.8 34.0 %shard_map.59 = (f32[19,16,16,128]{3,2,1,0:T(8,128)S(1)}, f32[1,16]{1,0:T(1,128)S(1)}) custom-call(f32[19,16,16,128]{3,2,1,0:T(8,128)S(1)} %copy-done, f32[16,16,128]{2,1,0:T(8,128)S(1)} %copy-done.2, s32[16,16,128]{2,1,0:T(8,128)S(1)} %copy-done.3, f32[19,16,16,128]{3,2,1,0:T(8,128)S(1)} %copy-done.1), custom_call_target="tpu_custom_call" | custom-call | tf_op jit(solution)/shard_map/pallas_call | solution.py:390
  39.9 1.5 %copy.8 = f32[19,16,16,128]{3,2,1,0:T(8,128)} copy(f32[19,16,16,128]{3,2,1,0:T(8,128)S(1)} %get-tuple-element.8) | data formatting | bytes 4980736
  41.3 0.5 %copy.9 = f32[16]{0:T(128)} copy(f32[16]{0:T(128)S(1)} %bitcast.1) | data formatting | bytes 128
Async XLA Ops:
  0.6 1.7 %copy-start = (f32[19,16,16,128]{3,2,1,0:T(8,128)S(1)}, f32[19,16,16,128]{3,2,1,0:T(8,128)}, u32[]{:S(2)}) copy-start(f32[19,16,16,128]{3,2,1,0:T(8,128)} %pop_hbm.1) | copy-start | bytes 7471108
  2.3 1.7 %copy-start.1 = (f32[19,16,16,128]{3,2,1,0:T(8,128)S(1)}, f32[19,16,16,128]{3,2,1,0:T(8,128)}, u32[]{:S(2)}) copy-start(f32[19,16,16,128]{3,2,1,0:T(8,128)} %cot_hbm.1) | copy-start | bytes 7471108
  4.0 0.9 %copy-start.2 = (f32[16,16,128]{2,1,0:T(8,128)S(1)}, f32[16,16,128]{2,1,0:T(8,128)}, u32[]{:S(2)}) copy-start(f32[16,16,128]{2,1,0:T(8,128)} %gray_hbm.1) | copy-start | bytes 393220
  4.9 0.9 %copy-start.3 = (s32[16,16,128]{2,1,0:T(8,128)S(1)}, s32[16,16,128]{2,1,0:T(8,128)}, u32[]{:S(2)}) copy-start(s32[16,16,128]{2,1,0:T(8,128)} %mask_hbm.1) | copy-start | bytes 393220
where the time goes:
time: 42 us; the launch traced here: 41.9 us
  Pallas kernels  34 us (81%)
  local copies, waits for them, and re-layouts  7.17 us (17%)
  between operations  0.65 us (2%)
    pallas_call x1, Pallas kernels, local(): pl.pallas_call(functools.partial(kernel, flows, spans), out_shape=(jax.Sh...  34 us
    unnamed x10, local copies, waits for them, and re-layouts  7.17 us

commit v1 on v0

v1 whole, which is shorter than its diff:
```python
import functools
import math

import jax
import jax.numpy as jnp
from jax import lax
from jax.experimental import pallas as pl
from jax.experimental.pallas import tpu as pltpu
from jax.sharding import PartitionSpec as P

VELOCITY = (
    (0, 0, 0),
    (1, 0, 0), (-1, 0, 0), (0, 1, 0), (0, -1, 0), (0, 0, 1), (0, 0, -1),
    (1, 1, 0), (-1, -1, 0), (1, -1, 0), (-1, 1, 0),
    (1, 0, 1), (-1, 0, -1), (1, 0, -1), (-1, 0, 1),
    (0, 1, 1), (0, -1, -1), (0, 1, -1), (0, -1, 1),
)
ORDER = (1, 7, 9, 11, 13, 2, 8, 10, 12, 14, 0, 3, 4, 5, 6, 15, 16, 17, 18)
SLOT = tuple(ORDER.index(i) for i in range(19))
X_GROUP = {1: 0, -1: 5}
Y_GROUP = {s: tuple(i for i in range(19) if VELOCITY[i][1] == s) for s in (1, -1)}
CORNER = {(1, 1): 7, (-1, -1): 8, (1, -1): 9, (-1, 1): 10}
CORNERS = ((1, 1), (-1, -1), (1, -1), (-1, 1))
PAIRS = ((1, 2), (3, 4), (5, 6), (7, 8), (9, 10), (11, 12), (13, 14), (15, 16), (17, 18))
RATE = 1.0 / 0.6 - 1.2
ENDS = ((0, 1), (0, 2), (1, 2))
Z_DIRS = tuple(i for i in range(19) if VELOCITY[i][2])
PITCH = 32
BASE = 8
NX = 16
NY = 16
NZ = 128
CHUNKS = 4


def split(f):
    even = [f[p] + f[m] for p, m in PAIRS]
    odd = [f[p] - f[m] for p, m in PAIRS]
    return even, odd


def sums(even, odd):
    plane = [even[3 + 2 * k] + even[4 + 2 * k] for k in range(3)]
    cross = [even[3 + 2 * k] - even[4 + 2 * k] for k in range(3)]
    plus = [odd[3 + 2 * k] + odd[4 + 2 * k] for k in range(3)]
    minus = [odd[3 + 2 * k] - odd[4 + 2 * k] for k in range(3)]
    first = [plus[0] + plus[1], minus[0] + plus[2], minus[1] + minus[2]]
    return plane, cross, first


def state_of(f):
    even, odd = split(f)
    plane, cross, first = sums(even, odd)
    j = [odd[a] + first[a] for a in range(3)]
    second = [even[0] + (plane[0] + plane[1]), even[1] + (plane[0] + plane[2]), even[2] + (plane[1] + plane[2])]
    rho = (f[0] + second[0]) + (even[1] + even[2]) + plane[2]
    inv = 1.0 / rho
    u = [entry * inv for entry in j]
    return even, odd, cross, j, second, rho, u


def join(even, odd):
    out = [None] * 19
    for k, (p, m) in enumerate(PAIRS):
        out[p] = even[k] + odd[k]
        out[m] = even[k] - odd[k]
    return out


def collide(f, share, open_voxel):
    even, odd, cross, j, second, rho, u = state_of(f)
    keep = 1.0 - share
    square = [j[a] * u[a] for a in range(3)]
    mixed = [j[0] * u[1], j[0] * u[2], j[1] * u[2]]
    base = rho - 1.5 * (square[0] + square[1] + square[2])
    third = rho * (1.0 / 3.0)
    lack = [second[a] - third - square[a] for a in range(3)]
    rest = 0.4 * base + RATE * (lack[0] + lack[1] + lack[2])
    base_axis = base * (1.0 / 15.0)
    base_edge = base * (1.0 / 30.0)
    grown = [0.15 * square[a] for a in range(3)]
    e_parts = [base_axis + 2.0 * grown[a] - (0.5 * RATE) * lack[a] for a in range(3)]
    o_parts = [0.2 * j[a] for a in range(3)]
    half = [0.1 * j[a] for a in range(3)]
    for k, (a, b) in enumerate(ENDS):
        common = base_edge + (grown[a] + grown[b])
        twist = (5.0 / 12.0) * mixed[k] - (0.25 * RATE) * cross[k]
        e_parts += [common + twist, common - twist]
        o_parts += [half[a] + half[b], half[a] - half[b]]
    drop = join(
        [jnp.where(open_voxel, 0.6 * even[k] - e_parts[k], 0.0) for k in range(9)],
        [jnp.where(open_voxel, -0.4 * odd[k] - o_parts[k], 0.0) for k in range(9)],
    )
    drop[0] = jnp.where(open_voxel, 1.2 * f[0] - rest, 0.0)
    post = [None] * 19
    post[0] = f[0] - keep * drop[0]
    for p, m in PAIRS:
        post[p] = f[m] - keep * drop[p]
        post[m] = f[p] - keep * drop[m]
    return post, drop, u


def pull_back(u, g, share, state=None):
    g_even, g_odd = split(g)
    g_plane, g_cross, g_first = sums(g_even, g_odd)
    keep = 1.0 - share
    k_even = 0.6 * share - 0.1
    k_odd = -0.4 * share - 0.1
    g_axes = g_even[0] + g_even[1] + g_even[2]
    g_edges = g_plane[0] + g_plane[1] + g_plane[2]
    weighted = g[0] * (1.0 / 3.0) + g_axes * (1.0 / 18.0) + g_edges * (1.0 / 36.0)
    both = [g_plane[0] + g_plane[1], g_plane[0] + g_plane[2], g_plane[1] + g_plane[2]]
    diag = [0.5 * g_even[a] - g[0] for a in range(3)]
    side = [0.25 * g_cross[k] for k in range(3)]
    flow = [0.2 * g_odd[a] + 0.1 * g_first[a] for a in range(3)]
    shared = 3.6 * weighted
    entry = [0.6 * g_even[a] + 0.3 * both[a] + (2.0 * RATE) * diag[a] - shared for a in range(3)]
    tilt = [(5.0 / 3.0) * side[k] for k in range(3)]
    turn = [
        u[0] * entry[0] + (tilt[0] * u[1] + tilt[1] * u[2]),
        u[1] * entry[1] + (tilt[0] * u[0] + tilt[2] * u[2]),
        u[2] * entry[2] + (tilt[1] * u[0] + tilt[2] * u[1]),
    ]
    scalar = 1.2 * weighted + (RATE / 3.0) * (diag[0] + diag[1] + diag[2])
    half_turn = [0.5 * turn[a] for a in range(3)]
    bar_rho = scalar - (u[0] * half_turn[0] + u[1] * half_turn[1] + u[2] * half_turn[2])
    grade = None
    if state is not None:
        even, odd, cross, j, second, rho, rest = state
        grade = 1.2 * (g[0] * rest) - rho * scalar
        for a in range(3):
            grade = grade - j[a] * (flow[a] + half_turn[a])
        bend = diag[0] * second[0] + diag[1] * second[1] + diag[2] * second[2]
        bend = bend + (side[0] * cross[0] + side[1] * cross[1] + side[2] * cross[2])
        dot_even = g_even[0] * even[0]
        dot_odd = g_odd[0] * odd[0]
        for k in range(1, 9):
            dot_even = dot_even + g_even[k] * even[k]
            dot_odd = dot_odd + g_odd[k] * odd[k]
        grade = grade + RATE * bend + (0.6 * dot_even - 0.4 * dot_odd)
    bar_rho = keep * bar_rho
    bar_j = [keep * (flow[a] + turn[a]) for a in range(3)]
    scale = keep * RATE
    diag = [scale * entry_a for entry_a in diag]
    side = [scale * entry_k for entry_k in side]
    e_parts = [bar_rho - diag[a] for a in range(3)]
    o_parts = list(bar_j)
    for k, (a, b) in enumerate(ENDS):
        common = e_parts[a] - diag[b]
        e_parts += [common - side[k], common + side[k]]
        o_parts += [bar_j[a] + bar_j[b], bar_j[a] - bar_j[b]]
    out = join(
        [k_even * g_even[k] + e_parts[k] for k in range(9)],
        [k_odd * g_odd[k] + o_parts[k] for k in range(9)],
    )
    out[0] = 2.0 * (k_even * g[0]) + bar_rho
    return out, grade


def lane_shift(value, step, lane):
    if step == 0:
        return value
    if step > 0:
        return jnp.where(lane == 0, 0.0, pltpu.roll(value, 1, 1))
    return jnp.where(lane == NZ - 1, 0.0, pltpu.roll(value, NZ - 1, 1))


class Field:
    def __init__(self, raw, shifted, y_send, y_recv, c_recv, sign, width, sends, recvs):
        self.raw, self.shifted = raw, shifted
        self.flat_raw = raw.reshape(19 * width, (NX + 2) * PITCH, NZ)
        self.flat_shifted = shifted.reshape(len(Z_DIRS) * width, (NX + 2) * PITCH, NZ)
        self.y_send, self.y_recv, self.c_recv = y_send, y_recv, c_recv
        self.sign, self.width, self.sends, self.recvs = sign, width, sends, recvs

    def slot(self, i, part=0):
        return self.width * SLOT[i] + part

    def z_slot(self, i, part=0):
        return self.width * Z_DIRS.index(i) + part

    def pick(self, i, part=0):
        if VELOCITY[i][2]:
            return self.shifted, self.flat_shifted, self.z_slot(i, part)
        return self.raw, self.flat_raw, self.slot(i, part)


def kernel(
    flows, spans,
    pop_hbm, gray_hbm, mask_hbm, cot_hbm,
    out_hbm, profile_ref,
    pop, gray, mask, speed,
    post_raw, post_z, cot_raw, cot_z, pre_raw, pre_z,
    post_ys, post_yr, post_cr, cot_ys, cot_yr, cot_cr, pre_ys, pre_yr, pre_cr,
    grades, y_grades, rows,
    in_sems, out_sem, send_sems, recv_sems, row_send, row_recv,
):
    fl = lax.axis_index("flow")
    sp = lax.axis_index("span")
    up = lax.rem(fl + 1, flows)
    down = lax.rem(fl + flows - 1, flows)
    flow_at = {1: up, -1: down}
    span_at = {1: sp + 1, -1: sp - 1}
    inside = {1: sp < spans - 1, -1: sp > 0}
    post = Field(post_raw, post_z, post_ys, post_yr, post_cr, 1, 2, send_sems.at[0], recv_sems.at[0])
    cot = Field(cot_raw, cot_z, cot_ys, cot_yr, cot_cr, -1, 1, send_sems.at[1], recv_sems.at[1])
    pre = Field(pre_raw, pre_z, pre_ys, pre_yr, pre_cr, -1, 1, send_sems.at[2], recv_sems.at[2])

    def target(step_x, step_y):
        return {
            "flow": flow_at[step_x] if step_x else fl,
            "span": span_at[step_y] if step_y else sp,
        }

    chunk = NX // CHUNKS
    pop_loads = [
        pltpu.make_async_copy(
            pop_hbm.at[:, pl.ds(chunk * c, chunk)], pop.at[:, pl.ds(chunk * c, chunk)], in_sems.at[c]
        )
        for c in range(CHUNKS)
    ]
    side_loads = [
        pltpu.make_async_copy(gray_hbm, gray, in_sems.at[CHUNKS]),
        pltpu.make_async_copy(mask_hbm, mask, in_sems.at[CHUNKS + 1]),
    ]
    cot_loads = [
        pltpu.make_async_copy(
            cot_hbm.at[ORDER[k]], cot_raw.at[k, pl.ds(1, NX), pl.ds(BASE, NY), :], in_sems.at[CHUNKS + 2 + k]
        )
        for k in range(19)
    ]
    pop_loads[0].start()
    for load in side_loads + pop_loads[1:] + cot_loads:
        load.start()

    steps = sorted(range(spans), key=lambda d: min(d, spans - d))
    peers = [(side, step) for step in steps for side in (0, 1, 2) if side or step]

    def peer(side, step):
        return {"flow": (fl, up, down)[side], "span": lax.rem(sp + step, spans) if step else sp}

    barrier = pltpu.get_barrier_semaphore()
    for side, step in peers:
        pl.semaphore_signal(barrier, inc=1, device_id=peer(side, step))

    def copies(field):
        buf, width, sign = field.raw, field.width, field.sign
        made = []

        def remote(src, dst, index, where, sent, received):
            copy = pltpu.make_async_remote_copy(
                src_ref=src,
                dst_ref=dst,
                send_sem=field.sends.at[index],
                recv_sem=field.recvs.at[index],
                device_id=where,
            )
            made.append((copy, sent, received))

        for n, (step_x, step_y) in enumerate(CORNERS):
            slot = field.slot(CORNER[(sign * step_x, sign * step_y)])
            plane = NX if step_x > 0 else 1
            row = BASE + (NY - 8 if step_y > 0 else 0)
            src = buf.at[pl.ds(slot, width), plane, pl.ds(row, 8), :]
            remote(src, field.c_recv.at[n], 4 + n, target(step_x, step_y), inside[step_y], inside[-step_y])
        for n, step in enumerate((1, -1)):
            remote(field.y_send.at[n], field.y_recv.at[n], 2 + n, target(0, step), inside[step], inside[-step])
        for n, step in enumerate((1, -1)):
            group = pl.ds(width * X_GROUP[sign * step], 5 * width)
            src = buf.at[group, NX if step > 0 else 1, pl.ds(BASE, NY), :]
            dst = buf.at[group, 0 if step > 0 else NX + 1, pl.ds(BASE, NY), :]
            remote(src, dst, n, target(step, 0), None, None)
        return made

    def send(field):
        for n, step in enumerate((1, -1)):
            row = PITCH + BASE + (NY - 1 if step > 0 else 0)
            for k, i in enumerate(Y_GROUP[field.sign * step]):
                for part in range(field.width):
                    field.y_send[n, field.width * k + part] = field.flat_raw[
                        field.slot(i, part), pl.ds(row, NX, stride=PITCH), :
                    ]
        made = copies(field)
        for copy, sent, _ in made:
            if sent is None:
                copy.start()
            else:
                pl.when(sent)(copy.start)
        return made

    lane = lax.broadcasted_iota(jnp.int32, (8, NZ), 1)
    wide_lane = lax.broadcasted_iota(jnp.int32, (NX, NZ), 1)
    row_at = lax.broadcasted_iota(jnp.int32, (8, NZ), 0)

    def receive(made, field):
        sign, width = field.sign, field.width
        for copy, _, received in made:
            if received is None:
                copy.wait_recv()
            else:
                pl.when(received)(copy.wait_recv)
        for n, step in enumerate((1, -1)):
            row = PITCH + BASE + (-1 if step > 0 else NY)

            def place(step=step, n=n, row=row, empty=False):
                for k, i in enumerate(Y_GROUP[sign * step]):
                    for part in range(width):
                        _, flat, slot = field.pick(i, part)
                        if empty:
                            value = jnp.zeros((NX, NZ), jnp.float32)
                        else:
                            value = lane_shift(field.y_recv[n, width * k + part], sign * VELOCITY[i][2], wide_lane)
                        flat[slot, pl.ds(row, NX, stride=PITCH), :] = value
                for m, (step_x, step_y) in enumerate(CORNERS):
                    if step_y != step:
                        continue
                    i = CORNER[(sign * step_x, sign * step_y)]
                    at = 7 if step_y > 0 else 0
                    plane = 0 if step_x > 0 else NX + 1
                    for part in range(width):
                        corner = jnp.zeros((1, NZ), jnp.float32) if empty else field.c_recv[m, part, pl.ds(at, 1), :]
                        field.raw[field.slot(i, part), plane, pl.ds(BASE + (-1 if step > 0 else NY), 1), :] = corner

            pl.when(inside[-step])(place)
            pl.when(jnp.logical_not(inside[-step]))(functools.partial(place, empty=True))
        for plane, step in ((0, 1), (NX + 1, -1)):
            for i in Z_DIRS:
                if VELOCITY[i][0] != sign * step:
                    continue
                for part in range(width):
                    for h in range(2):
                        field.shifted[field.z_slot(i, part), plane, pl.ds(BASE + 8 * h, 8), :] = lane_shift(
                            field.raw[field.slot(i, part), plane, pl.ds(BASE + 8 * h, 8), :],
                            sign * VELOCITY[i][2],
                            lane,
                        )

    def finish(made):
        for copy, sent, _ in made:
            if sent is None:
                copy.wait_send()
            else:
                pl.when(sent)(copy.wait_send)

    def shift_own(field):
        @pl.loop(0, NX // 4)
        def _(block):
            for part in range(field.width):
                values = []
                for i in Z_DIRS:
                    for q in range(4):
                        for h in range(2):
                            at = (4 * block + q + 1, pl.ds(BASE + 8 * h, 8))
                            value = field.raw[field.slot(i, part), at[0], at[1], :]
                            values.append((i, at, lane_shift(value, field.sign * VELOCITY[i][2], lane)))
                for i, at, value in values:
                    field.shifted[field.z_slot(i, part), at[0], at[1], :] = value

    def moved(field, tile, part=0):
        kind, at, h = tile
        values = []
        for i in range(19):
            step_x, step_y = field.sign * VELOCITY[i][0], field.sign * VELOCITY[i][1]
            ref, flat, slot = field.pick(i, part)
            if kind == "x":
                values.append(ref[slot, at + 1 - step_x, pl.ds(BASE + 8 * h - step_y, 8), :])
            else:
                start = (8 * h + 1 - step_x) * PITCH + BASE - step_y + at
                values.append(flat[slot, pl.ds(start, 8, stride=PITCH), :])
        return values

    def flat_of(ref):
        shape = ref.shape
        return ref.reshape(*shape[:-3], NX * NY, NZ)

    def own(ref, tile, *lead):
        kind, at, h = tile
        if kind == "x":
            return ref[(*lead, at, pl.ds(8 * h, 8), slice(None))]
        return flat_of(ref)[(*lead, pl.ds(8 * NY * h + at, 8, stride=NY), slice(None))]

    def share_of(tile):
        open_voxel = own(mask, tile) == 1
        return jnp.where(open_voxel, own(gray, tile), 1.0), open_voxel

    def first_half(tile):
        kind, at, h = tile
        f = moved(post, tile)
        even, odd, cross, j, second, rho, u = state_of(f)
        share, open_voxel = share_of(tile)
        out, grade = pull_back(u, moved(cot, tile), share, (even, odd, cross, j, second, rho, f[0]))
        centre = jnp.where(open_voxel, grade, 0.0)
        parts = [centre, None, None]
        for i, (value, drop) in enumerate(zip(out, moved(post, tile, 1))):
            index = (0, 1, 2)[VELOCITY[i][0]]
            term = value * drop
            parts[index] = term if parts[index] is None else parts[index] + term
        for i in range(19):
            if kind == "x":
                pre_raw[pre.slot(i), at + 1, pl.ds(BASE + 8 * h, 8), :] = out[i]
            else:
                start = (8 * h + 1) * PITCH + BASE + at
                pre.flat_raw[pre.slot(i), pl.ds(start, 8, stride=PITCH), :] = out[i]
        return parts

    def second_half(tile):
        kind, at, h = tile
        share, _ = share_of(tile)
        out, _ = pull_back([own(speed, tile, a) for a in range(3)], moved(pre, tile), share)
        for i in range(19):
            if kind == "x":
                pop[i, at, pl.ds(8 * h, 8), :] = out[i]
            else:
                flat_of(pop)[i, pl.ds(8 * NY * h + at, 8, stride=NY), :] = out[i]

    def without_edge(h, value):
        return jnp.where(row_at == 7 * h, 0.0, value)

    for load in side_loads:
        load.wait()

    def first_collision(x):
        for h in range(2):
            tile = ("x", x, h)
            share, open_voxel = share_of(tile)
            made, drop, u = collide([own(pop, tile, i) for i in range(19)], share, open_voxel)
            for i in range(19):
                post_raw[post.slot(i), x + 1, pl.ds(BASE + 8 * h, 8), :] = made[i]
                post_raw[post.slot(i, 1), x + 1, pl.ds(BASE + 8 * h, 8), :] = drop[i]
            for a in range(3):
                speed[a, x, pl.ds(8 * h, 8), :] = u[a]

    for c in range(CHUNKS):
        if c == CHUNKS - 1:
            pl.semaphore_wait(barrier, len(peers))
            for load in cot_loads:
                load.wait()
            cot_copies = send(cot)
        pop_loads[c].wait()

        @pl.loop(chunk * c, chunk * (c + 1))
        def _(x):
            first_collision(x)

    post_copies = send(post)
    shift_own(post)
    shift_own(cot)

    @pl.loop(1, NX - 1)
    def _(x):
        halves = [[without_edge(h, part) for part in first_half(("x", x, h))] for h in range(2)]
        for q in range(3):
            grades[q, x] = halves[0][q] + halves[1][q]

    receive(cot_copies, cot)
    receive(post_copies, post)

    @pl.loop(0, 2)
    def _(end):
        at = (NX - 1) * end
        halves = [first_half(("x", at, h)) for h in range(2)]
        for q in range(3):
            grades[q, at] = halves[0][q] + halves[1][q]
        for h in range(2):
            for q, part in enumerate(first_half(("y", at, h))):
                y_grades[end, q, pl.ds(8 * h, 8), :] = without_edge(h, part)

    pre_copies = send(pre)

    line = None
    row_index = lax.broadcasted_iota(jnp.int32, (NX, NZ), 0)
    for q, lead in enumerate((1, 0, 2)):
        part = jnp.sum(grades[q], axis=1) + (y_grades[0, q] + y_grades[1, q])
        part = jnp.sum(part, axis=1, keepdims=True)
        part = jnp.where(wide_lane == row_index + lead, part, 0.0)
        line = part if line is None else line + part
    rows[0, sp] = jnp.sum(line, axis=0, keepdims=True)
    row_copies = []
    for side, step in peers:
        copy = pltpu.make_async_remote_copy(
            src_ref=rows.at[0, sp],
            dst_ref=rows.at[side, sp],
            send_sem=row_send.at[side, step],
            recv_sem=row_recv.at[side, step],
            device_id=peer(side, step),
        )
        copy.start()
        row_copies.append(copy)

    shift_own(pre)

    @pl.loop(1, NX - 1)
    def _(x):
        for h in range(2):
            second_half(("x", x, h))

    receive(pre_copies, pre)

    @pl.loop(0, 2)
    def _(end):
        at = (NX - 1) * end
        for h in range(2):
            second_half(("x", at, h))
        for h in range(2):
            second_half(("y", at, h))

    out_copy = pltpu.make_async_copy(pop, out_hbm, out_sem)
    out_copy.start()
    finish(post_copies)
    finish(cot_copies)
    finish(pre_copies)
    for copy in row_copies:
        copy.wait_recv()
    one_lane = lax.broadcasted_iota(jnp.int32, (1, NZ), 1)
    total = jnp.sum(rows[0], axis=0)
    from_down = jnp.sum(rows[1], axis=0)
    from_up = jnp.sum(rows[2], axis=0)
    total = total + jnp.where(one_lane == 1, pltpu.roll(from_down, NZ - NX, 1), 0.0)
    total = total + jnp.where(one_lane == NX, pltpu.roll(from_up, NX, 1), 0.0)
    total = pltpu.roll(total, NZ - 1, 1) * (1.0 / math.sqrt(spans * NY * NZ))
    profile_ref[...] = total[:, :NX]
    for copy in row_copies:
        copy.wait_send()
    out_copy.wait()


def local(flows, spans, populations, gray, fluid_mask, cotangent):
    def vmem(*shape):
        return pltpu.VMEM(shape, jnp.float32)

    zs = len(Z_DIRS)
    faces = [vmem(2, 10, NX, NZ), vmem(2, 10, NX, NZ), vmem(4, 2, 8, NZ)]
    for _ in range(2):
        faces += [vmem(2, 5, NX, NZ), vmem(2, 5, NX, NZ), vmem(4, 1, 8, NZ)]
    adjoint, profile = pl.pallas_call(
        functools.partial(kernel, flows, spans),
        out_shape=(
            jax.ShapeDtypeStruct((19, NX, NY, NZ), jnp.float32),
            jax.ShapeDtypeStruct((1, NX), jnp.float32),
        ),
        in_specs=[pl.BlockSpec(memory_space=pl.ANY)] * 4,
        out_specs=(pl.BlockSpec(memory_space=pl.ANY), pl.BlockSpec(memory_space=pltpu.VMEM)),
        scratch_shapes=[
            vmem(19, NX, NY, NZ),
            vmem(NX, NY, NZ),
            pltpu.VMEM((NX, NY, NZ), jnp.int32),
            vmem(3, NX, NY, NZ),
            vmem(38, NX + 2, PITCH, NZ),
            vmem(2 * zs, NX + 2, PITCH, NZ),
            vmem(19, NX + 2, PITCH, NZ),
            vmem(zs, NX + 2, PITCH, NZ),
            vmem(19, NX + 2, PITCH, NZ),
            vmem(zs, NX + 2, PITCH, NZ),
            *faces,
            vmem(3, NX, 8, NZ),
            vmem(2, 3, NX, NZ),
            vmem(3, spans, 1, NZ),
            pltpu.SemaphoreType.DMA((CHUNKS + 21,)),
            pltpu.SemaphoreType.DMA,
            pltpu.SemaphoreType.DMA((3, 8)),
            pltpu.SemaphoreType.DMA((3, 8)),
            pltpu.SemaphoreType.DMA((3, spans)),
            pltpu.SemaphoreType.DMA((3, spans)),
        ],
        compiler_params=pltpu.CompilerParams(
            collective_id=0, has_side_effects=True, vmem_limit_bytes=60 * 1024 * 1024
        ),
    )(populations, gray, fluid_mask, cotangent)
    return adjoint, profile.reshape(NX)


def solution(mesh):
    placed = (
        P(None, "flow", "span", None),
        P("flow", "span", None),
        P("flow", "span", None),
        P(None, "flow", "span", None),
    )
    return jax.shard_map(
        functools.partial(local, mesh.shape["flow"], mesh.shape["span"]),
        mesh=mesh,
        in_specs=placed,
        out_specs=(P(None, "flow", "span", None), P("flow")),
        check_vma=False,
    )
```

time: 42 us -> 32.7 us (0.78)
  the two profiles are of different devices: /device:TPU:1 before, /device:TPU:24 now
where the time goes in v1:
time: 32.7 us; the launch traced here: 32.6 us
  Pallas kernels  28.1 us (86%)
  local copies, waits for them, and re-layouts  3.89 us (12%)
  between operations  0.65 us (2%)
    pallas_call x1, Pallas kernels, local(): pl.pallas_call(functools.partial(kernel, flows, spans), out_shape=(jax.Sh...  28.1 us
    unnamed x4, local copies, waits for them, and re-layouts  3.89 us

profile of v1, /device:TPU:24, one launch (start us, length us, event | category | flops | bytes accessed | tf_op | source)
XLA Modules:
  0.0 32.6 jit_solution(5313287869091935771)
XLA Ops:
  0.6 28.1 %shard_map.59 = (f32[19,16,16,128]{3,2,1,0:T(8,128)}, f32[1,16]{1,0:T(1,128)}) custom-call(f32[19,16,16,128]{3,2,1,0:T(8,128)} %pop_hbm.1, f32[16,16,128]{2,1,0:T(8,128)} %gray_hbm.1, s32[16,16,128]{2,1,0:T(8,128)} %mask_hbm.1, f32[19,16,16,128]{3,2,1,0:T(8,128)} %cot_hbm.1), custom_call_target="tpu_custom_call" | custom-call | tf_op jit(solution)/shard_map/pallas_call | solution.py:535
  28.7 0.0 copy-start
  28.7 3.4 %copy.8 = f32[19,16,16,128]{3,2,1,0:T(8,128)} copy(f32[19,16,16,128]{3,2,1,0:T(8,128)} %get-tuple-element.8) | data formatting | bytes 4980736
  32.1 0.0 copy-done
  32.1 0.5 %copy.9 = f32[16]{0:T(128)} copy(f32[16]{0:T(128)S(1)} %bitcast.1) | data formatting | bytes 128
Async XLA Ops:
  28.7 3.4 %copy-start = (f32[1,16]{1,0:T(1,128)S(1)}, f32[1,16]{1,0:T(1,128)}, u32[]{:S(2)}) copy-start(f32[1,16]{1,0:T(1,128)} %get-tuple-element.5) | copy-start | bytes 196

commit v2 on v1

--- a/solution.py
+++ b/solution.py
@@ -188,12 +188,12 @@
 def kernel(
     flows, spans,
     pop_hbm, gray_hbm, mask_hbm, cot_hbm,
-    out_hbm, profile_ref,
+    out_ref, profile_ref,
     pop, gray, mask, speed,
     post_raw, post_z, cot_raw, cot_z, pre_raw, pre_z,
     post_ys, post_yr, post_cr, cot_ys, cot_yr, cot_cr, pre_ys, pre_yr, pre_cr,
     grades, y_grades, rows,
-    in_sems, out_sem, send_sems, recv_sems, row_send, row_recv,
+    in_sems, send_sems, recv_sems, row_send, row_recv,
 ):
     fl = lax.axis_index("flow")
     sp = lax.axis_index("span")
@@ -272,7 +272,7 @@
             remote(src, dst, n, target(step, 0), None, None)
         return made
 
-    def send(field):
+    def pack(field):
         for n, step in enumerate((1, -1)):
             row = PITCH + BASE + (NY - 1 if step > 0 else 0)
             for k, i in enumerate(Y_GROUP[field.sign * step]):
@@ -280,12 +280,15 @@
                     field.y_send[n, field.width * k + part] = field.flat_raw[
                         field.slot(i, part), pl.ds(row, NX, stride=PITCH), :
                     ]
-        made = copies(field)
-        for copy, sent, _ in made:
-            if sent is None:
-                copy.start()
-            else:
-                pl.when(sent)(copy.start)
+
+    def send(*fields):
+        made = [copies(field) for field in fields]
+        for several in zip(*made):
+            for copy, sent, _ in several:
+                if sent is None:
+                    copy.start()
+                else:
+                    pl.when(sent)(copy.start)
         return made
 
     lane = lax.broadcasted_iota(jnp.int32, (8, NZ), 1)
@@ -409,9 +412,9 @@
         out, _ = pull_back([own(speed, tile, a) for a in range(3)], moved(pre, tile), share)
         for i in range(19):
             if kind == "x":
-                pop[i, at, pl.ds(8 * h, 8), :] = out[i]
+                out_ref[i, at, pl.ds(8 * h, 8), :] = out[i]
             else:
-                flat_of(pop)[i, pl.ds(8 * NY * h + at, 8, stride=NY), :] = out[i]
+                flat_of(out_ref)[i, pl.ds(8 * NY * h + at, 8, stride=NY), :] = out[i]
 
     def without_edge(h, value):
         return jnp.where(row_at == 7 * h, 0.0, value)
@@ -431,18 +434,18 @@
                 speed[a, x, pl.ds(8 * h, 8), :] = u[a]
 
     for c in range(CHUNKS):
-        if c == CHUNKS - 1:
-            pl.semaphore_wait(barrier, len(peers))
-            for load in cot_loads:
-                load.wait()
-            cot_copies = send(cot)
         pop_loads[c].wait()
 
         @pl.loop(chunk * c, chunk * (c + 1))
         def _(x):
             first_collision(x)
 
-    post_copies = send(post)
+    pack(post)
+    for load in cot_loads:
+        load.wait()
+    pack(cot)
+    pl.semaphore_wait(barrier, len(peers))
+    post_copies, cot_copies = send(post, cot)
     shift_own(post)
     shift_own(cot)
 
@@ -465,7 +468,8 @@
             for q, part in enumerate(first_half(("y", at, h))):
                 y_grades[end, q, pl.ds(8 * h, 8), :] = without_edge(h, part)
 
-    pre_copies = send(pre)
+    pack(pre)
+    (pre_copies,) = send(pre)
 
     line = None
     row_index = lax.broadcasted_iota(jnp.int32, (NX, NZ), 0)
@@ -504,8 +508,6 @@
         for h in range(2):
             second_half(("y", at, h))
 
-    out_copy = pltpu.make_async_copy(pop, out_hbm, out_sem)
-    out_copy.start()
     finish(post_copies)
     finish(cot_copies)
     finish(pre_copies)
@@ -521,7 +523,6 @@
     profile_ref[...] = total[:, :NX]
     for copy in row_copies:
         copy.wait_send()
-    out_copy.wait()
 
 
 def local(flows, spans, populations, gray, fluid_mask, cotangent):
@@ -539,7 +540,7 @@
             jax.ShapeDtypeStruct((1, NX), jnp.float32),
         ),
         in_specs=[pl.BlockSpec(memory_space=pl.ANY)] * 4,
-        out_specs=(pl.BlockSpec(memory_space=pl.ANY), pl.BlockSpec(memory_space=pltpu.VMEM)),
+        out_specs=(pl.BlockSpec(memory_space=pltpu.VMEM), pl.BlockSpec(memory_space=pltpu.VMEM)),
         scratch_shapes=[
             vmem(19, NX, NY, NZ),
             vmem(NX, NY, NZ),
@@ -556,16 +557,15 @@
             vmem(2, 3, NX, NZ),
             vmem(3, spans, 1, NZ),
             pltpu.SemaphoreType.DMA((CHUNKS + 21,)),
-            pltpu.SemaphoreType.DMA,
             pltpu.SemaphoreType.DMA((3, 8)),
             pltpu.SemaphoreType.DMA((3, 8)),
             pltpu.SemaphoreType.DMA((3, spans)),
             pltpu.SemaphoreType.DMA((3, spans)),
         ],
         compiler_params=pltpu.CompilerParams(
-            collective_id=0, has_side_effects=True, vmem_limit_bytes=60 * 1024 * 1024
+            collective_id=0, has_side_effects=True, vmem_limit_bytes=44 * 1024 * 1024
         ),
-    )(populations, gray, fluid_mask, cotangent)
+    )(*[pltpu.with_memory_space_constraint(x, pltpu.HBM) for x in (populations, gray, fluid_mask, cotangent)])
     return adjoint, profile.reshape(NX)
 
 

time: 32.7 us -> 29.5 us (0.902)
  the two profiles are of different devices: /device:TPU:24 before, /device:TPU:1 now
where the time goes in v2:
time: 29.5 us; the launch traced here: 29.4 us
  Pallas kernels  26.8 us (91%)
  local copies, waits for them, and re-layouts  1.96 us (7%)
  between operations  0.64 us (2%)
    pallas_call x1, Pallas kernels, local(): pl.pallas_call(functools.partial(kernel, flows, spans), out_shape=(jax.Sh...  26.8 us
    unnamed x2, local copies, waits for them, and re-layouts  1.96 us

profile of v2, /device:TPU:1, one launch (start us, length us, event | category | flops | bytes accessed | tf_op | source)
XLA Modules:
  0.0 29.4 jit_solution(6985739000317981514)
XLA Ops:
  0.6 26.8 %shard_map.59 = (f32[19,16,16,128]{3,2,1,0:T(8,128)S(1)}, f32[1,16]{1,0:T(1,128)S(1)}) custom-call(f32[19,16,16,128]{3,2,1,0:T(8,128)} %pop_hbm.1, f32[16,16,128]{2,1,0:T(8,128)} %gray_hbm.1, s32[16,16,128]{2,1,0:T(8,128)} %mask_hbm.1, f32[19,16,16,128]{3,2,1,0:T(8,128)} %cot_hbm.1), custom_call_target="tpu_custom_call" | custom-call | tf_op jit(solution)/shard_map/pallas_call | solution.py:536
  27.5 1.5 %copy.8 = f32[19,16,16,128]{3,2,1,0:T(8,128)} copy(f32[19,16,16,128]{3,2,1,0:T(8,128)S(1)} %get-tuple-element.8) | data formatting | bytes 4980736
  28.9 0.5 %copy.9 = f32[16]{0:T(128)} copy(f32[16]{0:T(128)S(1)} %bitcast.1) | data formatting | bytes 128

commit v3 on v2

--- a/solution.py
+++ b/solution.py
@@ -166,23 +166,17 @@
 
 
 class Field:
-    def __init__(self, raw, shifted, y_send, y_recv, c_recv, sign, width, sends, recvs):
+    def __init__(self, raw, shifted, y_send, y_recv, c_recv, sign, sends, recvs):
         self.raw, self.shifted = raw, shifted
-        self.flat_raw = raw.reshape(19 * width, (NX + 2) * PITCH, NZ)
-        self.flat_shifted = shifted.reshape(len(Z_DIRS) * width, (NX + 2) * PITCH, NZ)
+        self.flat_raw = raw.reshape(19, (NX + 2) * PITCH, NZ)
+        self.flat_shifted = shifted.reshape(len(Z_DIRS), (NX + 2) * PITCH, NZ)
         self.y_send, self.y_recv, self.c_recv = y_send, y_recv, c_recv
-        self.sign, self.width, self.sends, self.recvs = sign, width, sends, recvs
-
-    def slot(self, i, part=0):
-        return self.width * SLOT[i] + part
-
-    def z_slot(self, i, part=0):
-        return self.width * Z_DIRS.index(i) + part
-
-    def pick(self, i, part=0):
+        self.sign, self.sends, self.recvs = sign, sends, recvs
+
+    def pick(self, i):
         if VELOCITY[i][2]:
-            return self.shifted, self.flat_shifted, self.z_slot(i, part)
-        return self.raw, self.flat_raw, self.slot(i, part)
+            return self.shifted, self.flat_shifted, Z_DIRS.index(i)
+        return self.raw, self.flat_raw, SLOT[i]
 
 
 def kernel(
@@ -190,10 +184,10 @@
     pop_hbm, gray_hbm, mask_hbm, cot_hbm,
     out_ref, profile_ref,
     pop, gray, mask, speed,
-    post_raw, post_z, cot_raw, cot_z, pre_raw, pre_z,
-    post_ys, post_yr, post_cr, cot_ys, cot_yr, cot_cr, pre_ys, pre_yr, pre_cr,
+    post_raw, post_z, drop_raw, drop_z, cot_raw, cot_z, pre_raw, pre_z,
+    post_ys, post_yr, post_cr, drop_ys, drop_yr, drop_cr, cot_ys, cot_yr, cot_cr, pre_ys, pre_yr, pre_cr,
     grades, y_grades, rows,
-    in_sems, send_sems, recv_sems, row_send, row_recv,
+    in_sems, far_sems, send_sems, recv_sems, row_send, row_recv,
 ):
     fl = lax.axis_index("flow")
     sp = lax.axis_index("span")
@@ -202,9 +196,10 @@
     flow_at = {1: up, -1: down}
     span_at = {1: sp + 1, -1: sp - 1}
     inside = {1: sp < spans - 1, -1: sp > 0}
-    post = Field(post_raw, post_z, post_ys, post_yr, post_cr, 1, 2, send_sems.at[0], recv_sems.at[0])
-    cot = Field(cot_raw, cot_z, cot_ys, cot_yr, cot_cr, -1, 1, send_sems.at[1], recv_sems.at[1])
-    pre = Field(pre_raw, pre_z, pre_ys, pre_yr, pre_cr, -1, 1, send_sems.at[2], recv_sems.at[2])
+    post = Field(post_raw, post_z, post_ys, post_yr, post_cr, 1, send_sems.at[0], recv_sems.at[0])
+    cot = Field(cot_raw, cot_z, cot_ys, cot_yr, cot_cr, -1, send_sems.at[1], recv_sems.at[1])
+    pre = Field(pre_raw, pre_z, pre_ys, pre_yr, pre_cr, -1, send_sems.at[2], recv_sems.at[2])
+    drop = Field(drop_raw, drop_z, drop_ys, drop_yr, drop_cr, 1, send_sems.at[3], recv_sems.at[3])
 
     def target(step_x, step_y):
         return {
@@ -233,18 +228,50 @@
     for load in side_loads + pop_loads[1:] + cot_loads:
         load.start()
 
-    steps = sorted(range(spans), key=lambda d: min(d, spans - d))
+    steps = sorted(range(spans), key=lambda d: -min(d, spans - d))
     peers = [(side, step) for step in steps for side in (0, 1, 2) if side or step]
 
     def peer(side, step):
         return {"flow": (fl, up, down)[side], "span": lax.rem(sp + step, spans) if step else sp}
 
     barrier = pltpu.get_barrier_semaphore()
-    for side, step in peers:
-        pl.semaphore_signal(barrier, inc=1, device_id=peer(side, step))
+    for step_x in (1, -1):
+        pl.semaphore_signal(barrier, inc=1, device_id=target(step_x, 0))
+    for step_y in (1, -1):
+
+        @pl.when(inside[step_y])
+        def _():
+            for step_x in (1, -1, 0):
+                pl.semaphore_signal(barrier, inc=1, device_id=target(step_x, step_y))
+
+    def count_at(distance):
+        return (sp >= distance).astype(jnp.int32) + (sp + distance < spans).astype(jnp.int32)
+
+    def greet(semaphore, distance):
+        @pl.when(sp >= distance)
+        def _():
+            pl.semaphore_signal(semaphore, inc=1, device_id={"flow": fl, "span": sp - distance})
+
+        @pl.when(sp + distance < spans)
+        def _():
+            pl.semaphore_signal(semaphore, inc=1, device_id={"flow": fl, "span": sp + distance})
+
+    greet(barrier, 2)
+
+    distances = []
+    while 2 << len(distances) < spans:
+        distances.append(2 << len(distances))
+
+    def hear(stage):
+        if stage < len(distances):
+            pl.semaphore_wait(far_sems.at[stage], count_at(distances[stage]))
+
+    def tell(stage):
+        if stage < len(distances):
+            greet(far_sems.at[stage], distances[stage])
 
     def copies(field):
-        buf, width, sign = field.raw, field.width, field.sign
+        buf, sign = field.raw, field.sign
         made = []
 
         def remote(src, dst, index, where, sent, received):
@@ -258,15 +285,15 @@
             made.append((copy, sent, received))
 
         for n, (step_x, step_y) in enumerate(CORNERS):
-            slot = field.slot(CORNER[(sign * step_x, sign * step_y)])
+            slot = SLOT[CORNER[(sign * step_x, sign * step_y)]]
             plane = NX if step_x > 0 else 1
             row = BASE + (NY - 8 if step_y > 0 else 0)
-            src = buf.at[pl.ds(slot, width), plane, pl.ds(row, 8), :]
+            src = buf.at[slot, plane, pl.ds(row, 8), :]
             remote(src, field.c_recv.at[n], 4 + n, target(step_x, step_y), inside[step_y], inside[-step_y])
         for n, step in enumerate((1, -1)):
             remote(field.y_send.at[n], field.y_recv.at[n], 2 + n, target(0, step), inside[step], inside[-step])
         for n, step in enumerate((1, -1)):
-            group = pl.ds(width * X_GROUP[sign * step], 5 * width)
+            group = pl.ds(X_GROUP[sign * step], 5)
             src = buf.at[group, NX if step > 0 else 1, pl.ds(BASE, NY), :]
             dst = buf.at[group, 0 if step > 0 else NX + 1, pl.ds(BASE, NY), :]
             remote(src, dst, n, target(step, 0), None, None)
@@ -276,10 +303,7 @@
         for n, step in enumerate((1, -1)):
             row = PITCH + BASE + (NY - 1 if step > 0 else 0)
             for k, i in enumerate(Y_GROUP[field.sign * step]):
-                for part in range(field.width):
-                    field.y_send[n, field.width * k + part] = field.flat_raw[
-                        field.slot(i, part), pl.ds(row, NX, stride=PITCH), :
-                    ]
+                field.y_send[n, k] = field.flat_raw[SLOT[i], pl.ds(row, NX, stride=PITCH), :]
 
     def send(*fields):
         made = [copies(field) for field in fields]
@@ -296,7 +320,7 @@
     row_at = lax.broadcasted_iota(jnp.int32, (8, NZ), 0)
 
     def receive(made, field):
-        sign, width = field.sign, field.width
+        sign = field.sign
         for copy, _, received in made:
             if received is None:
                 copy.wait_recv()
@@ -307,22 +331,20 @@
 
             def place(step=step, n=n, row=row, empty=False):
                 for k, i in enumerate(Y_GROUP[sign * step]):
-                    for part in range(width):
-                        _, flat, slot = field.pick(i, part)
-                        if empty:
-                            value = jnp.zeros((NX, NZ), jnp.float32)
-                        else:
-                            value = lane_shift(field.y_recv[n, width * k + part], sign * VELOCITY[i][2], wide_lane)
-                        flat[slot, pl.ds(row, NX, stride=PITCH), :] = value
+                    _, flat, slot = field.pick(i)
+                    if empty:
+                        value = jnp.zeros((NX, NZ), jnp.float32)
+                    else:
+                        value = lane_shift(field.y_recv[n, k], sign * VELOCITY[i][2], wide_lane)
+                    flat[slot, pl.ds(row, NX, stride=PITCH), :] = value
                 for m, (step_x, step_y) in enumerate(CORNERS):
                     if step_y != step:
                         continue
                     i = CORNER[(sign * step_x, sign * step_y)]
                     at = 7 if step_y > 0 else 0
                     plane = 0 if step_x > 0 else NX + 1
-                    for part in range(width):
-                        corner = jnp.zeros((1, NZ), jnp.float32) if empty else field.c_recv[m, part, pl.ds(at, 1), :]
-                        field.raw[field.slot(i, part), plane, pl.ds(BASE + (-1 if step > 0 else NY), 1), :] = corner
+                    corner = jnp.zeros((1, NZ), jnp.float32) if empty else field.c_recv[m, pl.ds(at, 1), :]
+                    field.raw[SLOT[i], plane, pl.ds(BASE + (-1 if step > 0 else NY), 1), :] = corner
 
             pl.when(inside[-step])(place)
             pl.when(jnp.logical_not(inside[-step]))(functools.partial(place, empty=True))
@@ -330,13 +352,10 @@
             for i in Z_DIRS:
                 if VELOCITY[i][0] != sign * step:
                     continue
-                for part in range(width):
-                    for h in range(2):
-                        field.shifted[field.z_slot(i, part), plane, pl.ds(BASE + 8 * h, 8), :] = lane_shift(
-                            field.raw[field.slot(i, part), plane, pl.ds(BASE + 8 * h, 8), :],
-                            sign * VELOCITY[i][2],
-                            lane,
-                        )
+                for h in range(2):
+                    field.shifted[Z_DIRS.index(i), plane, pl.ds(BASE + 8 * h, 8), :] = lane_shift(
+                        field.raw[SLOT[i], plane, pl.ds(BASE + 8 * h, 8), :], sign * VELOCITY[i][2], lane
+                    )
 
     def finish(made):
         for copy, sent, _ in made:
@@ -348,23 +367,22 @@
     def shift_own(field):
         @pl.loop(0, NX // 4)
         def _(block):
-            for part in range(field.width):
-                values = []
-                for i in Z_DIRS:
-                    for q in range(4):
-                        for h in range(2):
-                            at = (4 * block + q + 1, pl.ds(BASE + 8 * h, 8))
-                            value = field.raw[field.slot(i, part), at[0], at[1], :]
-                            values.append((i, at, lane_shift(value, field.sign * VELOCITY[i][2], lane)))
-                for i, at, value in values:
-                    field.shifted[field.z_slot(i, part), at[0], at[1], :] = value
-
-    def moved(field, tile, part=0):
+            values = []
+            for i in Z_DIRS:
+                for q in range(4):
+                    for h in range(2):
+                        at = (4 * block + q + 1, pl.ds(BASE + 8 * h, 8))
+                        value = field.raw[SLOT[i], at[0], at[1], :]
+                        values.append((i, at, lane_shift(value, field.sign * VELOCITY[i][2], lane)))
+            for i, at, value in values:
+                field.shifted[Z_DIRS.index(i), at[0], at[1], :] = value
+
+    def moved(field, tile, which=range(19)):
         kind, at, h = tile
         values = []
-        for i in range(19):
+        for i in which:
             step_x, step_y = field.sign * VELOCITY[i][0], field.sign * VELOCITY[i][1]
-            ref, flat, slot = field.pick(i, part)
+            ref, flat, slot = field.pick(i)
             if kind == "x":
                 values.append(ref[slot, at + 1 - step_x, pl.ds(BASE + 8 * h - step_y, 8), :])
             else:
@@ -386,7 +404,19 @@
         open_voxel = own(mask, tile) == 1
         return jnp.where(open_voxel, own(gray, tile), 1.0), open_voxel
 
-    def first_half(tile):
+    def products(parts, values, tile, which):
+        for i, value in zip(which, moved(drop, tile, which)):
+            index = (0, 1, 2)[VELOCITY[i][0]]
+            term = values[i] * value
+            parts[index] = term if parts[index] is None else parts[index] + term
+
+    def late(tile):
+        kind, at, h = tile
+        at_end, at_half = (1 if at == 0 else -1), (1 if h == 0 else -1)
+        steps = (at_end, at_half) if kind == "x" else (at_half, at_end)
+        return [i for i in range(19) if VELOCITY[i][0] == steps[0] or VELOCITY[i][1] == steps[1]]
+
+    def first_half(tile, left=()):
         kind, at, h = tile
         f = moved(post, tile)
         even, odd, cross, j, second, rho, u = state_of(f)
@@ -394,16 +424,27 @@
         out, grade = pull_back(u, moved(cot, tile), share, (even, odd, cross, j, second, rho, f[0]))
         centre = jnp.where(open_voxel, grade, 0.0)
         parts = [centre, None, None]
-        for i, (value, drop) in enumerate(zip(out, moved(post, tile, 1))):
-            index = (0, 1, 2)[VELOCITY[i][0]]
-            term = value * drop
-            parts[index] = term if parts[index] is None else parts[index] + term
+        products(parts, out, tile, [i for i in range(19) if i not in left])
         for i in range(19):
             if kind == "x":
-                pre_raw[pre.slot(i), at + 1, pl.ds(BASE + 8 * h, 8), :] = out[i]
+                pre_raw[SLOT[i], at + 1, pl.ds(BASE + 8 * h, 8), :] = out[i]
             else:
                 start = (8 * h + 1) * PITCH + BASE + at
-                pre.flat_raw[pre.slot(i), pl.ds(start, 8, stride=PITCH), :] = out[i]
+                pre.flat_raw[SLOT[i], pl.ds(start, 8, stride=PITCH), :] = out[i]
+        return parts
+
+    def rest_of(tile):
+        kind, at, h = tile
+        which = late(tile)
+        values = {}
+        for i in which:
+            if kind == "x":
+                values[i] = pre_raw[SLOT[i], at + 1, pl.ds(BASE + 8 * h, 8), :]
+            else:
+                start = (8 * h + 1) * PITCH + BASE + at
+                values[i] = pre.flat_raw[SLOT[i], pl.ds(start, 8, stride=PITCH), :]
+        parts = [None, None, None]
+        products(parts, values, tile, which)
         return parts
 
     def second_half(tile):
@@ -426,10 +467,10 @@
         for h in range(2):
             tile = ("x", x, h)
             share, open_voxel = share_of(tile)
-            made, drop, u = collide([own(pop, tile, i) for i in range(19)], share, open_voxel)
+            made, lost, u = collide([own(pop, tile, i) for i in range(19)], share, open_voxel)
             for i in range(19):
-                post_raw[post.slot(i), x + 1, pl.ds(BASE + 8 * h, 8), :] = made[i]
-                post_raw[post.slot(i, 1), x + 1, pl.ds(BASE + 8 * h, 8), :] = drop[i]
+                post_raw[SLOT[i], x + 1, pl.ds(BASE + 8 * h, 8), :] = made[i]
+                drop_raw[SLOT[i], x + 1, pl.ds(BASE + 8 * h, 8), :] = lost[i]
             for a in range(3):
                 speed[a, x, pl.ds(8 * h, 8), :] = u[a]
 
@@ -444,10 +485,16 @@
     for load in cot_loads:
         load.wait()
     pack(cot)
-    pl.semaphore_wait(barrier, len(peers))
+    pl.semaphore_wait(barrier, 2 + 3 * count_at(1) + count_at(2))
     post_copies, cot_copies = send(post, cot)
+    tell(0)
+    pack(drop)
+    (drop_copies,) = send(drop)
     shift_own(post)
     shift_own(cot)
+    hear(0)
+    tell(1)
+    shift_own(drop)
 
     @pl.loop(1, NX - 1)
     def _(x):
@@ -455,21 +502,36 @@
         for q in range(3):
             grades[q, x] = halves[0][q] + halves[1][q]
 
+    hear(1)
+    tell(2)
     receive(cot_copies, cot)
     receive(post_copies, post)
 
-    @pl.loop(0, 2)
-    def _(end):
+    for end in (0, 1):
         at = (NX - 1) * end
-        halves = [first_half(("x", at, h)) for h in range(2)]
+        halves = [first_half(("x", at, h), late(("x", at, h))) for h in range(2)]
         for q in range(3):
-            grades[q, at] = halves[0][q] + halves[1][q]
+            both = [part[q] for part in halves if part[q] is not None]
+            grades[q, at] = functools.reduce(jnp.add, both) if both else jnp.zeros((8, NZ), jnp.float32)
         for h in range(2):
-            for q, part in enumerate(first_half(("y", at, h))):
-                y_grades[end, q, pl.ds(8 * h, 8), :] = without_edge(h, part)
+            for q, part in enumerate(first_half(("y", at, h), late(("y", at, h)))):
+                kept = jnp.zeros((8, NZ), jnp.float32) if part is None else without_edge(h, part)
+                y_grades[end, q, pl.ds(8 * h, 8), :] = kept
 
     pack(pre)
     (pre_copies,) = send(pre)
+    receive(drop_copies, drop)
+    for end in (0, 1):
+        at = (NX - 1) * end
+        shares = [rest_of(("x", at, h)) for h in range(2)]
+        for q in range(3):
+            both = [part[q] for part in shares if part[q] is not None]
+            if both:
+                grades[q, at] += functools.reduce(jnp.add, both)
+        for h in range(2):
+            for q, part in enumerate(rest_of(("y", at, h))):
+                if part is not None:
+                    y_grades[end, q, pl.ds(8 * h, 8), :] += without_edge(h, part)
 
     line = None
     row_index = lax.broadcasted_iota(jnp.int32, (NX, NZ), 0)
@@ -479,6 +541,7 @@
         part = jnp.where(wide_lane == row_index + lead, part, 0.0)
         line = part if line is None else line + part
     rows[0, sp] = jnp.sum(line, axis=0, keepdims=True)
+    hear(2)
     row_copies = []
     for side, step in peers:
         copy = pltpu.make_async_remote_copy(
@@ -509,6 +572,7 @@
             second_half(("y", at, h))
 
     finish(post_copies)
+    finish(drop_copies)
     finish(cot_copies)
     finish(pre_copies)
     for copy in row_copies:
@@ -530,9 +594,7 @@
         return pltpu.VMEM(shape, jnp.float32)
 
     zs = len(Z_DIRS)
-    faces = [vmem(2, 10, NX, NZ), vmem(2, 10, NX, NZ), vmem(4, 2, 8, NZ)]
-    for _ in range(2):
-        faces += [vmem(2, 5, NX, NZ), vmem(2, 5, NX, NZ), vmem(4, 1, 8, NZ)]
+    faces = [vmem(2, 5, NX, NZ), vmem(2, 5, NX, NZ), vmem(4, 8, NZ)] * 4
     adjoint, profile = pl.pallas_call(
         functools.partial(kernel, flows, spans),
         out_shape=(
@@ -546,19 +608,15 @@
             vmem(NX, NY, NZ),
             pltpu.VMEM((NX, NY, NZ), jnp.int32),
             vmem(3, NX, NY, NZ),
-            vmem(38, NX + 2, PITCH, NZ),
-            vmem(2 * zs, NX + 2, PITCH, NZ),
-            vmem(19, NX + 2, PITCH, NZ),
-            vmem(zs, NX + 2, PITCH, NZ),
-            vmem(19, NX + 2, PITCH, NZ),
-            vmem(zs, NX + 2, PITCH, NZ),
+            *[vmem(19, NX + 2, PITCH, NZ), vmem(zs, NX + 2, PITCH, NZ)] * 4,
             *faces,
             vmem(3, NX, 8, NZ),
             vmem(2, 3, NX, NZ),
             vmem(3, spans, 1, NZ),
             pltpu.SemaphoreType.DMA((CHUNKS + 21,)),
-            pltpu.SemaphoreType.DMA((3, 8)),
-            pltpu.SemaphoreType.DMA((3, 8)),
+            pltpu.SemaphoreType.REGULAR((4,)),
+            pltpu.SemaphoreType.DMA((4, 8)),
+            pltpu.SemaphoreType.DMA((4, 8)),
             pltpu.SemaphoreType.DMA((3, spans)),
             pltpu.SemaphoreType.DMA((3, spans)),
         ],

time: 29.5 us -> 28.6 us (0.969)
  Pallas kernels: 26.8 us -> 26 us
    pallas_call x1, Pallas kernels: 26.8 us -> 26 us  [local(): pl.pallas_call(functools.partial(kernel, flows, spans), out_shape=(jax.Sh...]
where the time goes in v3:
time: 28.6 us
  Pallas kernels  26 us (91%)
  local copies, waits for them, and re-layouts  1.96 us (7%)
  between operations  0.64 us (2%)
    pallas_call x1, Pallas kernels, local(): pl.pallas_call(functools.partial(kernel, flows, spans), out_shape=(jax.Sh...  26 us
    unnamed x2, local copies, waits for them, and re-layouts  1.96 us

profile of v3, /device:TPU:1, one launch (start us, length us, event | category | flops | bytes accessed | tf_op | source)
XLA Modules:
  0.0 28.6 jit_solution(17320068267321814880)
XLA Ops:
  0.6 26.0 %shard_map.59 = (f32[19,16,16,128]{3,2,1,0:T(8,128)S(1)}, f32[1,16]{1,0:T(1,128)S(1)}) custom-call(f32[19,16,16,128]{3,2,1,0:T(8,128)} %pop_hbm.1, f32[16,16,128]{2,1,0:T(8,128)} %gray_hbm.1, s32[16,16,128]{2,1,0:T(8,128)} %mask_hbm.1, f32[19,16,16,128]{3,2,1,0:T(8,128)} %cot_hbm.1), custom_call_target="tpu_custom_call" | custom-call | tf_op jit(solution)/shard_map/pallas_call | solution.py:598
  26.6 1.5 %copy.8 = f32[19,16,16,128]{3,2,1,0:T(8,128)} copy(f32[19,16,16,128]{3,2,1,0:T(8,128)S(1)} %get-tuple-element.8) | data formatting | bytes 4980736
  28.1 0.5 %copy.9 = f32[16]{0:T(128)} copy(f32[16]{0:T(128)S(1)} %bitcast.1) | data formatting | bytes 128

commit v4 on v3

--- a/solution.py
+++ b/solution.py
@@ -20,7 +20,6 @@
 X_GROUP = {1: 0, -1: 5}
 Y_GROUP = {s: tuple(i for i in range(19) if VELOCITY[i][1] == s) for s in (1, -1)}
 CORNER = {(1, 1): 7, (-1, -1): 8, (1, -1): 9, (-1, 1): 10}
-CORNERS = ((1, 1), (-1, -1), (1, -1), (-1, 1))
 PAIRS = ((1, 2), (3, 4), (5, 6), (7, 8), (9, 10), (11, 12), (13, 14), (15, 16), (17, 18))
 RATE = 1.0 / 0.6 - 1.2
 ENDS = ((0, 1), (0, 2), (1, 2))
@@ -30,7 +29,7 @@
 NX = 16
 NY = 16
 NZ = 128
-CHUNKS = 4
+CHUNKS = 2
 
 
 def split(f):
@@ -166,12 +165,12 @@
 
 
 class Field:
-    def __init__(self, raw, shifted, y_send, y_recv, c_recv, sign, sends, recvs):
-        self.raw, self.shifted = raw, shifted
+    def __init__(self, index, raw, shifted, y_send, y_recv, sign, recvs):
+        self.index, self.raw, self.shifted = index, raw, shifted
         self.flat_raw = raw.reshape(19, (NX + 2) * PITCH, NZ)
         self.flat_shifted = shifted.reshape(len(Z_DIRS), (NX + 2) * PITCH, NZ)
-        self.y_send, self.y_recv, self.c_recv = y_send, y_recv, c_recv
-        self.sign, self.sends, self.recvs = sign, sends, recvs
+        self.y_send, self.y_recv = y_send, y_recv
+        self.sign, self.recvs = sign, recvs
 
     def pick(self, i):
         if VELOCITY[i][2]:
@@ -185,9 +184,8 @@
     out_ref, profile_ref,
     pop, gray, mask, speed,
     post_raw, post_z, drop_raw, drop_z, cot_raw, cot_z, pre_raw, pre_z,
-    post_ys, post_yr, post_cr, drop_ys, drop_yr, drop_cr, cot_ys, cot_yr, cot_cr, pre_ys, pre_yr, pre_cr,
-    grades, y_grades, rows,
-    in_sems, far_sems, send_sems, recv_sems, row_send, row_recv,
+    y_send, y_recv, grades, y_grades, line_ref, rows,
+    in_sems, far_sems, send_sems, recv_sems, row_sems,
 ):
     fl = lax.axis_index("flow")
     sp = lax.axis_index("span")
@@ -196,10 +194,10 @@
     flow_at = {1: up, -1: down}
     span_at = {1: sp + 1, -1: sp - 1}
     inside = {1: sp < spans - 1, -1: sp > 0}
-    post = Field(post_raw, post_z, post_ys, post_yr, post_cr, 1, send_sems.at[0], recv_sems.at[0])
-    cot = Field(cot_raw, cot_z, cot_ys, cot_yr, cot_cr, -1, send_sems.at[1], recv_sems.at[1])
-    pre = Field(pre_raw, pre_z, pre_ys, pre_yr, pre_cr, -1, send_sems.at[2], recv_sems.at[2])
-    drop = Field(drop_raw, drop_z, drop_ys, drop_yr, drop_cr, 1, send_sems.at[3], recv_sems.at[3])
+    post = Field(0, post_raw, post_z, y_send.at[0], y_recv.at[0], 1, recv_sems.at[0])
+    cot = Field(1, cot_raw, cot_z, y_send.at[1], y_recv.at[1], -1, recv_sems.at[0])
+    drop = Field(2, drop_raw, drop_z, y_send.at[2], y_recv.at[2], 1, recv_sems.at[1])
+    pre = Field(3, pre_raw, pre_z, y_send.at[3], y_recv.at[3], -1, recv_sems.at[2])
 
     def target(step_x, step_y):
         return {
@@ -220,7 +218,7 @@
     ]
     cot_loads = [
         pltpu.make_async_copy(
-            cot_hbm.at[ORDER[k]], cot_raw.at[k, pl.ds(1, NX), pl.ds(BASE, NY), :], in_sems.at[CHUNKS + 2 + k]
+            cot_hbm.at[ORDER[k]], cot_raw.at[k, pl.ds(1, NX), pl.ds(BASE, NY), :], in_sems.at[CHUNKS + 2]
         )
         for k in range(19)
     ]
@@ -228,6 +226,9 @@
     for load in side_loads + pop_loads[1:] + cot_loads:
         load.start()
 
+    def take(ref, semaphore):
+        pltpu.make_async_copy(ref, ref, semaphore).wait()
+
     steps = sorted(range(spans), key=lambda d: -min(d, spans - d))
     peers = [(side, step) for step in steps for side in (0, 1, 2) if side or step]
 
@@ -272,32 +273,33 @@
 
     def copies(field):
         buf, sign = field.raw, field.sign
-        made = []
-
-        def remote(src, dst, index, where, sent, received):
-            copy = pltpu.make_async_remote_copy(
+        across, along = [], []
+
+        def remote(src, dst, index, where):
+            return pltpu.make_async_remote_copy(
                 src_ref=src,
                 dst_ref=dst,
-                send_sem=field.sends.at[index],
+                send_sem=send_sems.at[index],
                 recv_sem=field.recvs.at[index],
                 device_id=where,
             )
-            made.append((copy, sent, received))
-
-        for n, (step_x, step_y) in enumerate(CORNERS):
-            slot = SLOT[CORNER[(sign * step_x, sign * step_y)]]
-            plane = NX if step_x > 0 else 1
-            row = BASE + (NY - 8 if step_y > 0 else 0)
-            src = buf.at[slot, plane, pl.ds(row, 8), :]
-            remote(src, field.c_recv.at[n], 4 + n, target(step_x, step_y), inside[step_y], inside[-step_y])
+
         for n, step in enumerate((1, -1)):
-            remote(field.y_send.at[n], field.y_recv.at[n], 2 + n, target(0, step), inside[step], inside[-step])
+            for m, step_x in enumerate((1, -1)):
+                slot = SLOT[CORNER[(sign * step_x, sign * step)]]
+                plane = NX if step_x > 0 else 1
+                src = buf.at[slot, plane, pl.ds(BASE + (NY - 8 if step > 0 else 0), 8), :]
+                dst = field.y_recv.at[n, 5, pl.ds(8 * m, 8), :]
+                across.append((remote(src, dst, n, target(step_x, step)), inside[step]))
+        for n, step in enumerate((1, -1)):
+            src, dst = field.y_send.at[n], field.y_recv.at[n, pl.ds(0, 5)]
+            across.append((remote(src, dst, n, target(0, step)), inside[step]))
         for n, step in enumerate((1, -1)):
             group = pl.ds(X_GROUP[sign * step], 5)
             src = buf.at[group, NX if step > 0 else 1, pl.ds(BASE, NY), :]
             dst = buf.at[group, 0 if step > 0 else NX + 1, pl.ds(BASE, NY), :]
-            remote(src, dst, n, target(step, 0), None, None)
-        return made
+            along.append((remote(src, dst, 2, target(step, 0)), None))
+        return across, along
 
     def pack(field):
         for n, step in enumerate((1, -1)):
@@ -305,27 +307,26 @@
             for k, i in enumerate(Y_GROUP[field.sign * step]):
                 field.y_send[n, k] = field.flat_raw[SLOT[i], pl.ds(row, NX, stride=PITCH), :]
 
-    def send(*fields):
-        made = [copies(field) for field in fields]
-        for several in zip(*made):
-            for copy, sent, _ in several:
-                if sent is None:
-                    copy.start()
-                else:
-                    pl.when(sent)(copy.start)
-        return made
+    def send(*made):
+        for copy, sent in made:
+            if sent is None:
+                copy.start()
+            else:
+                pl.when(sent)(copy.start)
 
     lane = lax.broadcasted_iota(jnp.int32, (8, NZ), 1)
     wide_lane = lax.broadcasted_iota(jnp.int32, (NX, NZ), 1)
     row_at = lax.broadcasted_iota(jnp.int32, (8, NZ), 0)
 
-    def receive(made, field):
+    def arrive(*fields):
+        first, recvs = fields[0], fields[0].recvs
+        for n, step in enumerate((1, -1)):
+            came = y_recv.at[pl.ds(first.index, len(fields)), n]
+            pl.when(inside[-step])(functools.partial(take, came, recvs.at[n]))
+        take(first.raw.at[pl.ds(0, 10), pl.ds(0, len(fields)), pl.ds(BASE, NY), :], recvs.at[2])
+
+    def receive(field):
         sign = field.sign
-        for copy, _, received in made:
-            if received is None:
-                copy.wait_recv()
-            else:
-                pl.when(received)(copy.wait_recv)
         for n, step in enumerate((1, -1)):
             row = PITCH + BASE + (-1 if step > 0 else NY)
 
@@ -337,13 +338,11 @@
                     else:
                         value = lane_shift(field.y_recv[n, k], sign * VELOCITY[i][2], wide_lane)
                     flat[slot, pl.ds(row, NX, stride=PITCH), :] = value
-                for m, (step_x, step_y) in enumerate(CORNERS):
-                    if step_y != step:
-                        continue
-                    i = CORNER[(sign * step_x, sign * step_y)]
-                    at = 7 if step_y > 0 else 0
+                for m, step_x in enumerate((1, -1)):
+                    i = CORNER[(sign * step_x, sign * step)]
+                    at = 8 * m + (7 if step > 0 else 0)
                     plane = 0 if step_x > 0 else NX + 1
-                    corner = jnp.zeros((1, NZ), jnp.float32) if empty else field.c_recv[m, pl.ds(at, 1), :]
+                    corner = jnp.zeros((1, NZ), jnp.float32) if empty else field.y_recv[n, 5, pl.ds(at, 1), :]
                     field.raw[SLOT[i], plane, pl.ds(BASE + (-1 if step > 0 else NY), 1), :] = corner
 
             pl.when(inside[-step])(place)
@@ -357,12 +356,10 @@
                         field.raw[SLOT[i], plane, pl.ds(BASE + 8 * h, 8), :], sign * VELOCITY[i][2], lane
                     )
 
-    def finish(made):
-        for copy, sent, _ in made:
-            if sent is None:
-                copy.wait_send()
-            else:
-                pl.when(sent)(copy.wait_send)
+    def finish():
+        for n, step in enumerate((1, -1)):
+            pl.when(inside[step])(functools.partial(take, y_recv.at[:, n], send_sems.at[n]))
+        take(post_raw.at[pl.ds(0, 10), pl.ds(0, 4), pl.ds(BASE, NY), :], send_sems.at[2])
 
     def shift_own(field):
         @pl.loop(0, NX // 4)
@@ -457,6 +454,9 @@
             else:
                 flat_of(out_ref)[i, pl.ds(8 * NY * h + at, 8, stride=NY), :] = out[i]
 
+    def laid(tile, place):
+        return jnp.where(lane == place, jnp.sum(tile, axis=1, keepdims=True), 0.0)
+
     def without_edge(h, value):
         return jnp.where(row_at == 7 * h, 0.0, value)
 
@@ -482,14 +482,17 @@
             first_collision(x)
 
     pack(post)
-    for load in cot_loads:
-        load.wait()
+    pl.semaphore_wait(barrier, 2 + 3 * count_at(1) + count_at(2))
+    post_across, post_along = copies(post)
+    send(*post_across)
+    take(cot_raw.at[:, pl.ds(1, NX), pl.ds(BASE, NY), :], in_sems.at[CHUNKS + 2])
     pack(cot)
-    pl.semaphore_wait(barrier, 2 + 3 * count_at(1) + count_at(2))
-    post_copies, cot_copies = send(post, cot)
+    cot_across, cot_along = copies(cot)
+    send(*cot_across, *post_along, *cot_along)
     tell(0)
     pack(drop)
-    (drop_copies,) = send(drop)
+    drop_across, drop_along = copies(drop)
+    send(*drop_across, *drop_along)
     shift_own(post)
     shift_own(cot)
     hear(0)
@@ -502,10 +505,16 @@
         for q in range(3):
             grades[q, x] = halves[0][q] + halves[1][q]
 
+    line = jnp.zeros((8, NZ), jnp.float32)
+    for plane in range(NX):
+        terms = [grades[q, x] for q, x in enumerate((plane, plane + 1, plane - 1)) if 0 < x < NX - 1]
+        line = line + laid(functools.reduce(jnp.add, terms), plane + 1)
+    line_ref[...] = line
     hear(1)
     tell(2)
-    receive(cot_copies, cot)
-    receive(post_copies, post)
+    arrive(post, cot)
+    receive(cot)
+    receive(post)
 
     for end in (0, 1):
         at = (NX - 1) * end
@@ -519,8 +528,10 @@
                 y_grades[end, q, pl.ds(8 * h, 8), :] = kept
 
     pack(pre)
-    (pre_copies,) = send(pre)
-    receive(drop_copies, drop)
+    pre_across, pre_along = copies(pre)
+    send(*pre_across, *pre_along)
+    arrive(drop)
+    receive(drop)
     for end in (0, 1):
         at = (NX - 1) * end
         shares = [rest_of(("x", at, h)) for h in range(2)]
@@ -533,26 +544,23 @@
                 if part is not None:
                     y_grades[end, q, pl.ds(8 * h, 8), :] += without_edge(h, part)
 
-    line = None
-    row_index = lax.broadcasted_iota(jnp.int32, (NX, NZ), 0)
+    line = line_ref[...]
     for q, lead in enumerate((1, 0, 2)):
-        part = jnp.sum(grades[q], axis=1) + (y_grades[0, q] + y_grades[1, q])
-        part = jnp.sum(part, axis=1, keepdims=True)
-        part = jnp.where(wide_lane == row_index + lead, part, 0.0)
-        line = part if line is None else line + part
+        for at in (0, NX - 1):
+            line = line + laid(grades[q, at], at + lead)
+        for h in range(2):
+            part = y_grades[0, q, pl.ds(8 * h, 8), :] + y_grades[1, q, pl.ds(8 * h, 8), :]
+            line = line + laid(part, row_at + (8 * h + lead))
     rows[0, sp] = jnp.sum(line, axis=0, keepdims=True)
     hear(2)
-    row_copies = []
     for side, step in peers:
-        copy = pltpu.make_async_remote_copy(
+        pltpu.make_async_remote_copy(
             src_ref=rows.at[0, sp],
             dst_ref=rows.at[side, sp],
-            send_sem=row_send.at[side, step],
-            recv_sem=row_recv.at[side, step],
+            send_sem=row_sems.at[0],
+            recv_sem=row_sems.at[1],
             device_id=peer(side, step),
-        )
-        copy.start()
-        row_copies.append(copy)
+        ).start()
 
     shift_own(pre)
 
@@ -561,7 +569,8 @@
         for h in range(2):
             second_half(("x", x, h))
 
-    receive(pre_copies, pre)
+    arrive(pre)
+    receive(pre)
 
     @pl.loop(0, 2)
     def _(end):
@@ -571,12 +580,9 @@
         for h in range(2):
             second_half(("y", at, h))
 
-    finish(post_copies)
-    finish(drop_copies)
-    finish(cot_copies)
-    finish(pre_copies)
-    for copy in row_copies:
-        copy.wait_recv()
+    finish()
+    all_rows = rows.reshape(3 * spans, 1, NZ).at[pl.ds(0, len(peers))]
+    take(all_rows, row_sems.at[1])
     one_lane = lax.broadcasted_iota(jnp.int32, (1, NZ), 1)
     total = jnp.sum(rows[0], axis=0)
     from_down = jnp.sum(rows[1], axis=0)
@@ -585,8 +591,7 @@
     total = total + jnp.where(one_lane == NX, pltpu.roll(from_up, NX, 1), 0.0)
     total = pltpu.roll(total, NZ - 1, 1) * (1.0 / math.sqrt(spans * NY * NZ))
     profile_ref[...] = total[:, :NX]
-    for copy in row_copies:
-        copy.wait_send()
+    take(all_rows, row_sems.at[0])
 
 
 def local(flows, spans, populations, gray, fluid_mask, cotangent):
@@ -594,7 +599,6 @@
         return pltpu.VMEM(shape, jnp.float32)
 
     zs = len(Z_DIRS)
-    faces = [vmem(2, 5, NX, NZ), vmem(2, 5, NX, NZ), vmem(4, 8, NZ)] * 4
     adjoint, profile = pl.pallas_call(
         functools.partial(kernel, flows, spans),
         out_shape=(
@@ -609,16 +613,17 @@
             pltpu.VMEM((NX, NY, NZ), jnp.int32),
             vmem(3, NX, NY, NZ),
             *[vmem(19, NX + 2, PITCH, NZ), vmem(zs, NX + 2, PITCH, NZ)] * 4,
-            *faces,
+            vmem(4, 2, 5, NX, NZ),
+            vmem(4, 2, 6, NX, NZ),
             vmem(3, NX, 8, NZ),
             vmem(2, 3, NX, NZ),
+            vmem(8, NZ),
             vmem(3, spans, 1, NZ),
-            pltpu.SemaphoreType.DMA((CHUNKS + 21,)),
-            pltpu.SemaphoreType.REGULAR((4,)),
-            pltpu.SemaphoreType.DMA((4, 8)),
-            pltpu.SemaphoreType.DMA((4, 8)),
-            pltpu.SemaphoreType.DMA((3, spans)),
-            pltpu.SemaphoreType.DMA((3, spans)),
+            pltpu.SemaphoreType.DMA((CHUNKS + 3,)),
+            pltpu.SemaphoreType.REGULAR((3,)),
+            pltpu.SemaphoreType.DMA((3,)),
+            pltpu.SemaphoreType.DMA((3, 3)),
+            pltpu.SemaphoreType.DMA((2,)),
         ],
         compiler_params=pltpu.CompilerParams(
             collective_id=0, has_side_effects=True, vmem_limit_bytes=44 * 1024 * 1024

time: 28.6 us -> 27.2 us (0.951)
  Pallas kernels: 26 us -> 24.5 us
    pallas_call x1, Pallas kernels: 26 us -> 24.5 us  [local(): pl.pallas_call(functools.partial(kernel, flows, spans), out_shape=(jax.Sh...]
where the time goes in v4:
time: 27.2 us; the launch traced here: 27.1 us
  Pallas kernels  24.5 us (90%)
  local copies, waits for them, and re-layouts  1.96 us (7%)
  between operations  0.64 us (2%)
    pallas_call x1, Pallas kernels, local(): pl.pallas_call(functools.partial(kernel, flows, spans), out_shape=(jax.Sh...  24.5 us
    unnamed x2, local copies, waits for them, and re-layouts  1.96 us

profile of v4, /device:TPU:1, one launch (start us, length us, event | category | flops | bytes accessed | tf_op | source)
XLA Modules:
  0.0 27.1 jit_solution(15731850758432377960)
XLA Ops:
  0.6 24.5 %shard_map.59 = (f32[19,16,16,128]{3,2,1,0:T(8,128)S(1)}, f32[1,16]{1,0:T(1,128)S(1)}) custom-call(f32[19,16,16,128]{3,2,1,0:T(8,128)} %pop_hbm.1, f32[16,16,128]{2,1,0:T(8,128)} %gray_hbm.1, s32[16,16,128]{2,1,0:T(8,128)} %mask_hbm.1, f32[19,16,16,128]{3,2,1,0:T(8,128)} %cot_hbm.1), custom_call_target="tpu_custom_call" | custom-call | tf_op jit(solution)/shard_map/pallas_call | solution.py:602
  25.1 1.5 %copy.8 = f32[19,16,16,128]{3,2,1,0:T(8,128)} copy(f32[19,16,16,128]{3,2,1,0:T(8,128)S(1)} %get-tuple-element.8) | data formatting | bytes 4980736
  26.6 0.5 %copy.9 = f32[16]{0:T(128)} copy(f32[16]{0:T(128)S(1)} %bitcast.1) | data formatting | bytes 128

commit v5 on v4

--- a/solution.py
+++ b/solution.py
@@ -185,7 +185,7 @@
     pop, gray, mask, speed,
     post_raw, post_z, drop_raw, drop_z, cot_raw, cot_z, pre_raw, pre_z,
     y_send, y_recv, grades, y_grades, line_ref, rows,
-    in_sems, far_sems, send_sems, recv_sems, row_sems,
+    in_sems, far_sem, send_sems, recv_sems, row_sems,
 ):
     fl = lax.axis_index("flow")
     sp = lax.axis_index("span")
@@ -235,6 +235,19 @@
     def peer(side, step):
         return {"flow": (fl, up, down)[side], "span": lax.rem(sp + step, spans) if step else sp}
 
+    order = sorted(range(spans), key=lambda s: (min(s % 8, 4), s))
+    place_of = [order.index(s) for s in range(spans)]
+    my_place = functools.reduce(jnp.add, [place_of[s] * (sp == s).astype(jnp.int32) for s in range(spans)])
+
+    def far(s):
+        return ((s - sp) * (s - sp) > 1).astype(jnp.int32)
+
+    def before(s):
+        return (my_place > place_of[s]).astype(jnp.int32) * far(s)
+
+    def after(s):
+        return (my_place < place_of[s]).astype(jnp.int32) * far(s)
+
     barrier = pltpu.get_barrier_semaphore()
     for step_x in (1, -1):
         pl.semaphore_signal(barrier, inc=1, device_id=target(step_x, 0))
@@ -245,31 +258,29 @@
             for step_x in (1, -1, 0):
                 pl.semaphore_signal(barrier, inc=1, device_id=target(step_x, step_y))
 
+    for s in order[::-1]:
+
+        @pl.when(after(s) == 1)
+        def _():
+            for side in (fl, up, down):
+                pl.semaphore_signal(barrier, inc=1, device_id={"flow": side, "span": s})
+
     def count_at(distance):
         return (sp >= distance).astype(jnp.int32) + (sp + distance < spans).astype(jnp.int32)
 
-    def greet(semaphore, distance):
-        @pl.when(sp >= distance)
+    def tell():
+        for s in order:
+
+            @pl.when(before(s) == 1)
+            def _():
+                pl.semaphore_signal(far_sem, inc=1, device_id={"flow": fl, "span": s})
+
+    def hear():
+        later = functools.reduce(jnp.add, [after(s) for s in range(spans)])
+
+        @pl.when(later > 0)
         def _():
-            pl.semaphore_signal(semaphore, inc=1, device_id={"flow": fl, "span": sp - distance})
-
-        @pl.when(sp + distance < spans)
-        def _():
-            pl.semaphore_signal(semaphore, inc=1, device_id={"flow": fl, "span": sp + distance})
-
-    greet(barrier, 2)
-
-    distances = []
-    while 2 << len(distances) < spans:
-        distances.append(2 << len(distances))
-
-    def hear(stage):
-        if stage < len(distances):
-            pl.semaphore_wait(far_sems.at[stage], count_at(distances[stage]))
-
-    def tell(stage):
-        if stage < len(distances):
-            greet(far_sems.at[stage], distances[stage])
+            pl.semaphore_wait(far_sem, later)
 
     def copies(field):
         buf, sign = field.raw, field.sign
@@ -482,21 +493,19 @@
             first_collision(x)
 
     pack(post)
-    pl.semaphore_wait(barrier, 2 + 3 * count_at(1) + count_at(2))
+    pl.semaphore_wait(barrier, 2 + 3 * (count_at(1) + functools.reduce(jnp.add, [before(s) for s in range(spans)])))
     post_across, post_along = copies(post)
     send(*post_across)
     take(cot_raw.at[:, pl.ds(1, NX), pl.ds(BASE, NY), :], in_sems.at[CHUNKS + 2])
     pack(cot)
     cot_across, cot_along = copies(cot)
     send(*cot_across, *post_along, *cot_along)
-    tell(0)
+    tell()
     pack(drop)
     drop_across, drop_along = copies(drop)
     send(*drop_across, *drop_along)
     shift_own(post)
     shift_own(cot)
-    hear(0)
-    tell(1)
     shift_own(drop)
 
     @pl.loop(1, NX - 1)
@@ -510,8 +519,6 @@
         terms = [grades[q, x] for q, x in enumerate((plane, plane + 1, plane - 1)) if 0 < x < NX - 1]
         line = line + laid(functools.reduce(jnp.add, terms), plane + 1)
     line_ref[...] = line
-    hear(1)
-    tell(2)
     arrive(post, cot)
     receive(cot)
     receive(post)
@@ -552,7 +559,7 @@
             part = y_grades[0, q, pl.ds(8 * h, 8), :] + y_grades[1, q, pl.ds(8 * h, 8), :]
             line = line + laid(part, row_at + (8 * h + lead))
     rows[0, sp] = jnp.sum(line, axis=0, keepdims=True)
-    hear(2)
+    hear()
     for side, step in peers:
         pltpu.make_async_remote_copy(
             src_ref=rows.at[0, sp],
@@ -620,7 +627,7 @@
             vmem(8, NZ),
             vmem(3, spans, 1, NZ),
             pltpu.SemaphoreType.DMA((CHUNKS + 3,)),
-            pltpu.SemaphoreType.REGULAR((3,)),
+            pltpu.SemaphoreType.REGULAR,
             pltpu.SemaphoreType.DMA((3,)),
             pltpu.SemaphoreType.DMA((3, 3)),
             pltpu.SemaphoreType.DMA((2,)),

time: 27.2 us -> 26 us (0.956)
  Pallas kernels: 24.5 us -> 23.3 us
    pallas_call x1, Pallas kernels: 24.5 us -> 23.3 us  [local(): pl.pallas_call(functools.partial(kernel, flows, spans), out_shape=(jax.Sh...]
where the time goes in v5:
time: 26 us; the launch traced here: 25.9 us
  Pallas kernels  23.3 us (90%)
  local copies, waits for them, and re-layouts  1.96 us (8%)
  between operations  0.64 us (2%)
    pallas_call x1, Pallas kernels, local(): pl.pallas_call(functools.partial(kernel, flows, spans), out_shape=(jax.Sh...  23.3 us
    unnamed x2, local copies, waits for them, and re-layouts  1.96 us

profile of v5, /device:TPU:1, one launch (start us, length us, event | category | flops | bytes accessed | tf_op | source)
XLA Modules:
  0.0 25.9 jit_solution(2312992910667205803)
XLA Ops:
  0.6 23.3 %shard_map.59 = (f32[19,16,16,128]{3,2,1,0:T(8,128)S(1)}, f32[1,16]{1,0:T(1,128)S(1)}) custom-call(f32[19,16,16,128]{3,2,1,0:T(8,128)} %pop_hbm.1, f32[16,16,128]{2,1,0:T(8,128)} %gray_hbm.1, s32[16,16,128]{2,1,0:T(8,128)} %mask_hbm.1, f32[19,16,16,128]{3,2,1,0:T(8,128)} %cot_hbm.1), custom_call_target="tpu_custom_call" | custom-call | tf_op jit(solution)/shard_map/pallas_call | solution.py:609
  24.0 1.5 %copy.8 = f32[19,16,16,128]{3,2,1,0:T(8,128)} copy(f32[19,16,16,128]{3,2,1,0:T(8,128)S(1)} %get-tuple-element.8) | data formatting | bytes 4980736
  25.4 0.5 %copy.9 = f32[16]{0:T(128)} copy(f32[16]{0:T(128)S(1)} %bitcast.1) | data formatting | bytes 128

commit v6 on v5

--- a/solution.py
+++ b/solution.py
@@ -184,7 +184,7 @@
     out_ref, profile_ref,
     pop, gray, mask, speed,
     post_raw, post_z, drop_raw, drop_z, cot_raw, cot_z, pre_raw, pre_z,
-    y_send, y_recv, grades, y_grades, line_ref, rows,
+    y_send, y_recv, dense, grades, y_grades, line_ref, rows,
     in_sems, far_sem, send_sems, recv_sems, row_sems,
 ):
     fl = lax.axis_index("flow")
@@ -349,6 +349,8 @@
                     else:
                         value = lane_shift(field.y_recv[n, k], sign * VELOCITY[i][2], wide_lane)
                     flat[slot, pl.ds(row, NX, stride=PITCH), :] = value
+                    if field.index < 2:
+                        dense[field.index, n, i, pl.ds(BASE, NX), :] = value
                 for m, step_x in enumerate((1, -1)):
                     i = CORNER[(sign * step_x, sign * step)]
                     at = 8 * m + (7 if step > 0 else 0)
@@ -385,6 +387,16 @@
             for i, at, value in values:
                 field.shifted[Z_DIRS.index(i), at[0], at[1], :] = value
 
+    def gather(field):
+        for end in (0, 1):
+            for i in range(19):
+                step_y = field.sign * VELOCITY[i][1]
+                if step_y == 1 - 2 * end:
+                    continue
+                _, flat, slot = field.pick(i)
+                row = PITCH + BASE + (NY - 1) * end - step_y
+                dense[field.index, end, i, pl.ds(BASE, NX), :] = flat[slot, pl.ds(row, NX, stride=PITCH), :]
+
     def moved(field, tile, which=range(19)):
         kind, at, h = tile
         values = []
@@ -393,6 +405,8 @@
             ref, flat, slot = field.pick(i)
             if kind == "x":
                 values.append(ref[slot, at + 1 - step_x, pl.ds(BASE + 8 * h - step_y, 8), :])
+            elif field.index < 2:
+                values.append(dense[field.index, int(at > 0), i, pl.ds(BASE + 8 * h - step_x, 8), :])
             else:
                 start = (8 * h + 1 - step_x) * PITCH + BASE - step_y + at
                 values.append(flat[slot, pl.ds(start, 8, stride=PITCH), :])
@@ -505,7 +519,9 @@
     drop_across, drop_along = copies(drop)
     send(*drop_across, *drop_along)
     shift_own(post)
+    gather(post)
     shift_own(cot)
+    gather(cot)
     shift_own(drop)
 
     @pl.loop(1, NX - 1)
@@ -525,15 +541,16 @@
 
     for end in (0, 1):
         at = (NX - 1) * end
+        for h in range(2):
+            for q, part in enumerate(first_half(("y", at, h), late(("y", at, h)))):
+                kept = jnp.zeros((8, NZ), jnp.float32) if part is None else without_edge(h, part)
+                y_grades[end, q, pl.ds(8 * h, 8), :] = kept
+    for end in (0, 1):
+        at = (NX - 1) * end
         halves = [first_half(("x", at, h), late(("x", at, h))) for h in range(2)]
         for q in range(3):
             both = [part[q] for part in halves if part[q] is not None]
             grades[q, at] = functools.reduce(jnp.add, both) if both else jnp.zeros((8, NZ), jnp.float32)
-        for h in range(2):
-            for q, part in enumerate(first_half(("y", at, h), late(("y", at, h)))):
-                kept = jnp.zeros((8, NZ), jnp.float32) if part is None else without_edge(h, part)
-                y_grades[end, q, pl.ds(8 * h, 8), :] = kept
-
     pack(pre)
     pre_across, pre_along = copies(pre)
     send(*pre_across, *pre_along)
@@ -622,6 +639,7 @@
             *[vmem(19, NX + 2, PITCH, NZ), vmem(zs, NX + 2, PITCH, NZ)] * 4,
             vmem(4, 2, 5, NX, NZ),
             vmem(4, 2, 6, NX, NZ),
+            vmem(2, 2, 19, PITCH, NZ),
             vmem(3, NX, 8, NZ),
             vmem(2, 3, NX, NZ),
             vmem(8, NZ),

time: 26 us -> 25.7 us (0.988)
  Pallas kernels: 23.3 us -> 23 us
    pallas_call x1, Pallas kernels: 23.3 us -> 23 us  [local(): pl.pallas_call(functools.partial(kernel, flows, spans), out_shape=(jax.Sh...]
where the time goes in v6:
time: 25.7 us; the launch traced here: 25.6 us
  Pallas kernels  23 us (89%)
  local copies, waits for them, and re-layouts  1.96 us (8%)
  between operations  0.64 us (2%)
    pallas_call x1, Pallas kernels, local(): pl.pallas_call(functools.partial(kernel, flows, spans), out_shape=(jax.Sh...  23 us
    unnamed x2, local copies, waits for them, and re-layouts  1.96 us

profile of v6, /device:TPU:1, one launch (start us, length us, event | category | flops | bytes accessed | tf_op | source)
XLA Modules:
  0.0 25.6 jit_solution(11952028077455124515)
XLA Ops:
  0.6 23.0 %shard_map.59 = (f32[19,16,16,128]{3,2,1,0:T(8,128)S(1)}, f32[1,16]{1,0:T(1,128)S(1)}) custom-call(f32[19,16,16,128]{3,2,1,0:T(8,128)} %pop_hbm.1, f32[16,16,128]{2,1,0:T(8,128)} %gray_hbm.1, s32[16,16,128]{2,1,0:T(8,128)} %mask_hbm.1, f32[19,16,16,128]{3,2,1,0:T(8,128)} %cot_hbm.1), custom_call_target="tpu_custom_call" | custom-call | tf_op jit(solution)/shard_map/pallas_call | solution.py:626
  23.7 1.5 %copy.8 = f32[19,16,16,128]{3,2,1,0:T(8,128)} copy(f32[19,16,16,128]{3,2,1,0:T(8,128)S(1)} %get-tuple-element.8) | data formatting | bytes 4980736
  25.1 0.5 %copy.9 = f32[16]{0:T(128)} copy(f32[16]{0:T(128)S(1)} %bitcast.1) | data formatting | bytes 128
